TPU v7x, 256 devices: a whole 4x4x8 slice. The times are simulated.
256 devices in a mesh: row: 32 (over x_lo, z, core), col: 4 (over y), rep: 2 (over x_hi).
Axes of the slice: x: 4 (x_hi: 2, x_lo: 2; x = x_hi * 2 + x_lo), y: 4, z: 8, core: 2. Of those that a mesh axis runs over, the one named last changes fastest.
Arguments:
- queries: bfloat16 [131072, 768], P(('rep', 'row', 'col')), parts along dimension 0, may hold values from -16 to 16
- passages: bfloat16 [98304, 768], P(('rep', 'row', 'col')), parts along dimension 0, may hold values from -16 to 16
- positive: int32 [131072], P(('rep', 'row', 'col')), parts along dimension 0, may hold values from 0 to 383
- block_mask: int32 [131072, 15], P(('rep', 'row', 'col')), parts along dimension 0, may hold values from 0 to 1
- roster: int32 [131072, 3], P(('rep', 'row', 'col')), parts along dimension 0, may hold values from 0 to 2
Outputs:
- loss: float32 [2], P('rep'), parts along dimension 0
- grad_queries: float32 [131072, 768], P(('rep', 'row', 'col')), parts along dimension 0
- grad_passages: float32 [98304, 768], P(('rep', 'row', 'col')), parts along dimension 0
There are 2 independent parts, one for each index of `rep`. A program takes and returns all parts, laid end to end along the dimension named above; each array names one. Nothing has to cross between parts.
All inputs are finite; a program needn't handle non-finite values.
Results may differ from a plain program's by a relative error of at most 0.002.
Values may be sent and summed in bfloat16 or wider, within the bound.
A program may use at most 128 MiB of HBM per device.

v0:
```python
import jax
import jax.numpy as jnp
from jax import lax
from jax.sharding import PartitionSpec as P

BLK = 128


LOWEST = -1e30


def from_behind(block, axis, distance):
    devices = range(lax.axis_size(axis))
    route = [((i - distance) % len(devices), i) for i in devices]
    return lax.ppermute(block, axis, route)


def block_scores(query_rows, block_rows):
    scale = query_rows.shape[1] ** (-0.5)
    return (
        lax.dot_general(
            query_rows, block_rows, (((1,), (1,)), ((), ())), preferred_element_type=jnp.float32
        )
        * scale
    )


def forward_block(running, query_rows, block_rows, visible, target):
    highest, summed, positive_score = running
    scores = block_scores(query_rows, block_rows)
    masked = jnp.where(visible[:, None], scores, LOWEST)
    raised = jnp.maximum(highest, jnp.max(masked, axis=1))
    summed = summed * jnp.exp(highest - raised) + jnp.sum(
        jnp.where(visible[:, None], jnp.exp(scores - raised[:, None]), 0.0), axis=1
    )
    if target is not None:
        positive_score = positive_score + jnp.sum(jnp.where(target, scores, 0.0), axis=1)
    return (raised, summed, positive_score)


def backward_block(query_rows, block_rows, visible, target, log_total):
    scale = query_rows.shape[1] ** (-0.5)
    scores = block_scores(query_rows, block_rows)
    weights = jnp.where(visible[:, None], jnp.exp(scores - log_total[:, None]), 0.0)
    if target is not None:
        weights = weights - target.astype(jnp.float32)
    weights = weights.astype(jnp.bfloat16)
    toward = jnp.dot(weights, block_rows, preferred_element_type=jnp.float32)
    gradient = (
        lax.dot_general(
            weights, query_rows, (((0,), (0,)), ((), ())), preferred_element_type=jnp.float32
        )
        * scale
    )
    return (toward, gradient)


def sparse_forward(running, query_rows, block_rows, visible):
    return forward_block(running, query_rows, block_rows, visible, None)


def sparse_backward(query_rows, block_rows, visible, log_total):
    return backward_block(query_rows, block_rows, visible, None, log_total)


def cell_backward(query_rows, cell_rows, visible_list, target_list, log_total):
    toward_sum = jnp.zeros((query_rows.shape[0], cell_rows.shape[1]), jnp.float32)
    pieces = []
    for block_at, visible in enumerate(visible_list):
        block_rows = cell_rows[block_at * BLK : (block_at + 1) * BLK]
        if target_list is None:
            toward, gradient = sparse_backward(query_rows, block_rows, visible, log_total)
        else:
            toward, gradient = backward_block(
                query_rows, block_rows, visible, target_list[block_at], log_total
            )
        toward_sum = toward_sum + toward
        pieces.append(gradient)
    return (toward_sum, jnp.concatenate(pieces, axis=0))


def roll_cells(cell_rows, offset):
    return from_behind(cell_rows, "col", offset)


def roll_terms(gradient, offset):
    return from_behind(gradient, "col", offset)


def local(queries, passages, positive, block_mask, roster):
    n_row = lax.axis_size("row")
    n_col = lax.axis_size("col")
    reach = min(2, (n_row - 1) // 2)
    offsets = list(range(-reach, 0)) + list(range(1, reach + 1))
    blocks = passages.shape[0] // BLK
    scale = queries.shape[1] ** (-0.5)
    near_rows = [from_behind(passages, "row", -offset) for offset in offsets]
    random_rows = {}
    current = passages
    for stride in range(1, n_col):
        current = roll_cells(current, 1)
        random_rows[stride] = current
    column_ids = jnp.arange(BLK, dtype=jnp.int32)
    target_block = positive // BLK
    own_visible = [
        (block_mask[:, block_at] == 1) | (target_block == block_at) for block_at in range(blocks)
    ]
    own_target = [
        (block_at * BLK + column_ids)[None, :] == positive[:, None] for block_at in range(blocks)
    ]
    near_visible = [
        [block_mask[:, (group_at + 1) * blocks + block_at] == 1 for block_at in range(blocks)]
        for group_at in range(len(offsets))
    ]
    random_visible = {}
    for stride in range(1, n_col):
        random_visible[stride] = [roster[:, stride - 1] == block_at for block_at in range(blocks)]
    count = queries.shape[0]
    running = (
        jnp.full((count,), LOWEST, jnp.float32),
        jnp.zeros((count,), jnp.float32),
        jnp.zeros((count,), jnp.float32),
    )
    for block_at in range(blocks):
        running = forward_block(
            running,
            queries,
            passages[block_at * BLK : (block_at + 1) * BLK],
            own_visible[block_at],
            own_target[block_at],
        )
    for group_at in range(len(offsets)):
        for block_at in range(blocks):
            running = sparse_forward(
                running,
                queries,
                near_rows[group_at][block_at * BLK : (block_at + 1) * BLK],
                near_visible[group_at][block_at],
            )
    for stride in range(1, n_col):
        for block_at in range(blocks):
            running = sparse_forward(
                running,
                queries,
                random_rows[stride][block_at * BLK : (block_at + 1) * BLK],
                random_visible[stride][block_at],
            )
    highest, summed, positive_score = running
    log_total = highest + jnp.log(summed)
    loss_total = lax.psum(jnp.sum(log_total - positive_score), ("row", "col"))
    loss = (loss_total / (count * n_row * n_col)).reshape(1)
    toward_total, own_gradient = cell_backward(
        queries, passages, own_visible, own_target, log_total
    )
    near_gradients = []
    for group_at in range(len(offsets)):
        toward, gradient = cell_backward(
            queries, near_rows[group_at], near_visible[group_at], None, log_total
        )
        toward_total = toward_total + toward
        near_gradients.append(gradient)
    random_gradients = {}
    for stride in range(1, n_col):
        toward, gradient = cell_backward(
            queries, random_rows[stride], random_visible[stride], None, log_total
        )
        toward_total = toward_total + toward
        random_gradients[stride] = gradient
    returned = jnp.zeros_like(own_gradient)
    for offset, gradient in zip(offsets, near_gradients):
        returned = returned + from_behind(gradient, "row", offset)
    arrived = jnp.zeros_like(own_gradient)
    for stride in range(n_col - 1, 0, -1):
        arrived = roll_terms(random_gradients[stride] + arrived, -1)
    grad_queries = toward_total * scale
    grad_passages = own_gradient + returned + arrived
    return (loss, grad_queries, grad_passages)


def solution(mesh):
    return jax.shard_map(
        local,
        mesh=mesh,
        in_specs=(
            P(("rep", "row", "col"), None),
            P(("rep", "row", "col"), None),
            P(("rep", "row", "col")),
            P(("rep", "row", "col"), None),
            P(("rep", "row", "col"), None),
        ),
        out_specs=(P("rep"), P(("rep", "row", "col"), None), P(("rep", "row", "col"), None)),
        check_vma=False,
    )
```

profile of v0, /device:TPU:1, one launch (start us, length us, event | category | flops | bytes accessed | tf_op | source)
XLA Modules:
  0.0 435.3 jit_solution(15341185683323044152)
XLA Ops:
  0.6 3.3 collective-permute-start.2
  6.8 6.4 %collective-permute-start.3 = (bf16[384,768]{1,0:T(8,128)(2,1)}, bf16[384,768]{1,0:T(8,128)(2,1)S(1)}, u32[]{:S(2)}, u32[]{:S(2)}) collective-permute-start(bf16[384,768]{1,0:T(8,128)(2,1)} %param.6), channel_id=1, source_target_pairs={{16,0},{24,8},{32,16},{40,24},{48,32},{56,40},{64,48},{72,56},{80,... | collective-permute-start | bytes 1769480 | tf_op jit(solution)/shard_map/ppermute | solution.py:15
  22.5 9.6 %collective-permute-done = bf16[384,768]{1,0:T(8,128)(2,1)S(1)} collective-permute-done((bf16[384,768]{1,0:T(8,128)(2,1)}, bf16[384,768]{1,0:T(8,128)(2,1)S(1)}, u32[]{:S(2)}, u32[]{:S(2)}) %collective-permute-start) | collective-permute-done | bytes 589856 | tf_op jit(solution)/shard_map/ppermute | solution.py:15
  37.1 8.0 %collective-permute-done.5 = bf16[384,768]{1,0:T(8,128)(2,1)S(1)} collective-permute-done((bf16[384,768]{1,0:T(8,128)(2,1)S(1)}, bf16[384,768]{1,0:T(8,128)(2,1)S(1)}, u32[]{:S(2)}, u32[]{:S(2)}) %collective-permute-start.5) | collective-permute-done | bytes 589856 | tf_op jit(solution)/shard_map/ppermute | solution.py:15
  47.7 10.3 %collective-permute-done.6 = bf16[384,768]{1,0:T(8,128)(2,1)S(1)} collective-permute-done((bf16[384,768]{1,0:T(8,128)(2,1)S(1)}, bf16[384,768]{1,0:T(8,128)(2,1)S(1)}, u32[]{:S(2)}, u32[]{:S(2)}) %collective-permute-start.6) | collective-permute-done | bytes 589856 | tf_op jit(solution)/shard_map/ppermute | solution.py:15
  73.8 1.9 collective-permute-start.7
  77.9 1.7 collective-permute-start.9
  84.0 1.6 fusion.63
  85.5 1.6 fusion.60
  87.1 1.5 fusion.57
  90.2 1.6 fusion.51
  91.9 1.6 fusion.48
  93.4 1.6 fusion.45
  96.6 1.6 fusion.39
  98.1 1.6 fusion.36
  99.7 1.6 fusion.33
  103.1 1.6 fusion.27
  104.7 1.6 fusion.24
  113.3 287.8 %psum.7 = f32[]{:T(128)} all-reduce(f32[]{:T(128)} %get-tuple-element.37), channel_id=1, replica_groups=mesh['row'=32,'col'=4,'rep'=2] {'row','col'}, use_global_device_ids=true, to_apply=%region_52.53 | all-reduce | flops 1 | bytes 8 | tf_op jit(solution)/shard_map/psum | solution.py:150
  401.8 2.7 fusion.12
  406.0 2.9 maximum_add_fusion.1
  409.0 9.2 %add_multiply_fusion = f32[512,768]{1,0:T(8,128)} fusion(f32[512,768]{1,0:T(8,128)} %fusion.15, f32[512,768]{1,0:T(8,128)} %fusion.12, f32[512,768]{1,0:T(8,128)} %fusion.18, f32[512,768]{1,0:T(8,128)} %fusion.24, f32[512,768]{1,0:T(8,128)} %fusion.21, f32[512,768]{1,0:T(8,128)} %fusion.27, f32[512,768]{1,0:T(8,128)} %fusion.33, f32[512,768]{1,0:T(8,128)} %fusion.30, ...), kind=kOutput, calls=%fused_computation | convolution fusion | flops 110297088 | bytes 38210048 | tf_op jit(solution)/shard_map/dot_general | solution.py:48
  418.2 11.7 %collective-permute-done.13 = f32[384,768]{1,0:T(8,128)} collective-permute-done((f32[384,768]{1,0:T(8,128)}, f32[384,768]{1,0:T(8,128)}, u32[]{:S(2)}, u32[]{:S(2)}) %collective-permute-start.13) | collective-permute-done | bytes 1179680 | tf_op jit(solution)/shard_map/ppermute | solution.py:15
  429.9 4.3 fusion
  (137 shorter events, 55.0 us)
Async XLA Ops:
  0.6 15.3 %copy-start = (bf16[512,768]{1,0:T(8,128)(2,1)S(1)}, bf16[512,768]{1,0:T(8,128)(2,1)}, u32[]{:S(2)}) copy-start(bf16[512,768]{1,0:T(8,128)(2,1)} %param.5) | copy-start | bytes 2359300
  0.6 19.3 %collective-permute-start.2 = (bf16[384,768]{1,0:T(8,128)(2,1)}, bf16[384,768]{1,0:T(8,128)(2,1)S(1)}, u32[]{:S(2)}, u32[]{:S(2)}) collective-permute-start(bf16[384,768]{1,0:T(8,128)(2,1)} %param.6), channel_id=1, source_target_pairs={{8,0},{16,8},{24,16},{32,24},{40,32},{48,40},{56,48},{64,56},{72,6... | collective-permute-start | bytes 1769480 | tf_op jit(solution)/shard_map/ppermute | solution.py:15
  4.0 17.3 %collective-permute-start.1 = (bf16[384,768]{1,0:T(8,128)(2,1)}, bf16[384,768]{1,0:T(8,128)(2,1)S(1)}, u32[]{:S(2)}, u32[]{:S(2)}) collective-permute-start(bf16[384,768]{1,0:T(8,128)(2,1)} %param.6), channel_id=1, source_target_pairs={{248,0},{0,8},{8,16},{16,24},{24,32},{32,40},{40,48},{48,56},{56,6... | collective-permute-start | bytes 1769480 | tf_op jit(solution)/shard_map/ppermute | solution.py:15
  4.0 28.1 %collective-permute-start = (bf16[384,768]{1,0:T(8,128)(2,1)}, bf16[384,768]{1,0:T(8,128)(2,1)S(1)}, u32[]{:S(2)}, u32[]{:S(2)}) collective-permute-start(bf16[384,768]{1,0:T(8,128)(2,1)} %param.6), channel_id=1, source_target_pairs={{240,0},{248,8},{0,16},{8,24},{16,32},{24,40},{32,48},{40,56},{48,... | collective-permute-start | bytes 1769480 | tf_op jit(solution)/shard_map/ppermute | solution.py:15
  5.5 27.8 %collective-permute-start.4 = (bf16[384,768]{1,0:T(8,128)(2,1)}, bf16[384,768]{1,0:T(8,128)(2,1)S(1)}, u32[]{:S(2)}, u32[]{:S(2)}) collective-permute-start(bf16[384,768]{1,0:T(8,128)(2,1)} %param.6), channel_id=1, source_target_pairs={{6,0},{0,2},{2,4},{4,6},{7,1},{1,3},{3,5},{5,7},{14,8},{8,10},{10,... | collective-permute-start | bytes 1769480 | tf_op jit(solution)/shard_map/ppermute | solution.py:15
  6.8 29.1 %collective-permute-start.3 = (bf16[384,768]{1,0:T(8,128)(2,1)}, bf16[384,768]{1,0:T(8,128)(2,1)S(1)}, u32[]{:S(2)}, u32[]{:S(2)}) collective-permute-start(bf16[384,768]{1,0:T(8,128)(2,1)} %param.6), channel_id=1, source_target_pairs={{16,0},{24,8},{32,16},{40,24},{48,32},{56,40},{64,48},{72,56},{80,... | collective-permute-start | bytes 1769480 | tf_op jit(solution)/shard_map/ppermute | solution.py:15
  33.3 11.9 %collective-permute-start.5 = (bf16[384,768]{1,0:T(8,128)(2,1)S(1)}, bf16[384,768]{1,0:T(8,128)(2,1)S(1)}, u32[]{:S(2)}, u32[]{:S(2)}) collective-permute-start(bf16[384,768]{1,0:T(8,128)(2,1)S(1)} %collective-permute-done.4), channel_id=1, source_target_pairs={{6,0},{0,2},{2,4},{4,6},{7,1},{1,3},{3,5},{5,7},{14,8},{8,10},{10,... | collective-permute-start | bytes 1769480 | tf_op jit(solution)/shard_map/ppermute | solution.py:15
  45.1 12.8 %collective-permute-start.6 = (bf16[384,768]{1,0:T(8,128)(2,1)S(1)}, bf16[384,768]{1,0:T(8,128)(2,1)S(1)}, u32[]{:S(2)}, u32[]{:S(2)}) collective-permute-start(bf16[384,768]{1,0:T(8,128)(2,1)S(1)} %collective-permute-done.5), channel_id=1, source_target_pairs={{6,0},{0,2},{2,4},{4,6},{7,1},{1,3},{3,5},{5,7},{14,8},{8,10},{10,... | collective-permute-start | bytes 1769480 | tf_op jit(solution)/shard_map/ppermute | solution.py:15
  57.9 53.8 %copy-start.13 = (bf16[384,768]{1,0:T(8,128)(2,1)}, bf16[384,768]{1,0:T(8,128)(2,1)S(1)}, u32[]{:S(2)}) copy-start(bf16[384,768]{1,0:T(8,128)(2,1)S(1)} %collective-permute-done.6) | copy-start | bytes 1769476
  58.8 5.1 %copy-start.7 = (f32[512,128]{0,1:T(8,128)}, f32[512,128]{0,1:T(8,128)S(1)}, u32[]{:S(2)}) copy-start(f32[512,128]{0,1:T(8,128)S(1)} %get-tuple-element.69) | copy-start | bytes 786436
  73.8 344.4 %collective-permute-start.7 = (f32[384,768]{1,0:T(8,128)}, f32[384,768]{1,0:T(8,128)}, u32[]{:S(2)}, u32[]{:S(2)}) collective-permute-start(f32[384,768]{1,0:T(8,128)} %pad_maximum_fusion), channel_id=1, source_target_pairs={{16,0},{24,8},{32,16},{40,24},{48,32},{56,40},{64,48},{72,56},{80,... | collective-permute-start | bytes 3538952 | tf_op jit(solution)/shard_map/ppermute | solution.py:15
  76.8 341.4 %collective-permute-start.8 = (f32[384,768]{1,0:T(8,128)}, f32[384,768]{1,0:T(8,128)}, u32[]{:S(2)}, u32[]{:S(2)}) collective-permute-start(f32[384,768]{1,0:T(8,128)} %pad_maximum_fusion.1), channel_id=1, source_target_pairs={{8,0},{16,8},{24,16},{32,24},{40,32},{48,40},{56,48},{64,56},{72,6... | collective-permute-start | bytes 3538952 | tf_op jit(solution)/shard_map/ppermute | solution.py:15
  77.9 340.3 %collective-permute-start.9 = (f32[384,768]{1,0:T(8,128)}, f32[384,768]{1,0:T(8,128)}, u32[]{:S(2)}, u32[]{:S(2)}) collective-permute-start(f32[384,768]{1,0:T(8,128)} %pad_maximum_fusion.2), channel_id=1, source_target_pairs={{248,0},{0,8},{8,16},{16,24},{24,32},{32,40},{40,48},{48,56},{56,6... | collective-permute-start | bytes 3538952 | tf_op jit(solution)/shard_map/ppermute | solution.py:15
  80.7 337.4 %collective-permute-start.10 = (f32[384,768]{1,0:T(8,128)}, f32[384,768]{1,0:T(8,128)}, u32[]{:S(2)}, u32[]{:S(2)}) collective-permute-start(f32[384,768]{1,0:T(8,128)} %pad_maximum_fusion.3), channel_id=1, source_target_pairs={{240,0},{248,8},{0,16},{8,24},{16,32},{24,40},{32,48},{40,56},{48,... | collective-permute-start | bytes 3538952 | tf_op jit(solution)/shard_map/ppermute | solution.py:15
  80.8 28.6 %collective-permute-start.11 = (f32[384,768]{1,0:T(8,128)S(1)}, f32[384,768]{1,0:T(8,128)S(1)}, u32[]{:S(2)}, u32[]{:S(2)}) collective-permute-start(f32[384,768]{1,0:T(8,128)S(1)} %pad_maximum_fusion.4), channel_id=1, source_target_pairs={{2,0},{4,2},{6,4},{0,6},{3,1},{5,3},{7,5},{1,7},{10,8},{12,10},{14... | collective-permute-start | bytes 3538952 | tf_op jit(solution)/shard_map/ppermute | solution.py:15
  110.6 295.4 %collective-permute-start.12 = (f32[384,768]{1,0:T(8,128)}, f32[384,768]{1,0:T(8,128)}, u32[]{:S(2)}, u32[]{:S(2)}) collective-permute-start(f32[384,768]{1,0:T(8,128)} %maximum_add_fusion.2), channel_id=1, source_target_pairs={{2,0},{4,2},{6,4},{0,6},{3,1},{5,3},{7,5},{1,7},{10,8},{12,10},{14... | collective-permute-start | bytes 3538952 | tf_op jit(solution)/shard_map/ppermute | solution.py:15
  401.7 4.2 copy-start.10
  401.7 4.2 copy-start.11
  401.8 4.2 copy-start.12
  404.5 4.4 %copy-start.5 = (f32[512,768]{1,0:T(8,128)S(1)}, f32[512,768]{1,0:T(8,128)}, u32[]{:S(2)}) copy-start(f32[512,768]{1,0:T(8,128)} %fusion.54) | copy-start | bytes 4718596
  404.5 4.4 %copy-start.6 = (f32[512,768]{1,0:T(8,128)S(1)}, f32[512,768]{1,0:T(8,128)}, u32[]{:S(2)}) copy-start(f32[512,768]{1,0:T(8,128)} %fusion.51) | copy-start | bytes 4718596
  408.9 21.0 %copy-start.8 = (f32[128,768]{1,0:T(8,128)S(1)}, f32[128,768]{1,0:T(8,128)}, u32[]{:S(2)}) copy-start(f32[128,768]{1,0:T(8,128)} %convolution_multiply_fusion.21) | copy-start | bytes 1179652
  408.9 21.0 %copy-start.9 = (f32[128,768]{1,0:T(8,128)S(1)}, f32[128,768]{1,0:T(8,128)}, u32[]{:S(2)}) copy-start(f32[128,768]{1,0:T(8,128)} %convolution_multiply_fusion.23) | copy-start | bytes 1179652
  408.9 21.0 %collective-permute-start.13 = (f32[384,768]{1,0:T(8,128)}, f32[384,768]{1,0:T(8,128)}, u32[]{:S(2)}, u32[]{:S(2)}) collective-permute-start(f32[384,768]{1,0:T(8,128)} %maximum_add_fusion.1), channel_id=1, source_target_pairs={{2,0},{4,2},{6,4},{0,6},{3,1},{5,3},{7,5},{1,7},{10,8},{12,10},{14... | collective-permute-start | bytes 3538952 | tf_op jit(solution)/shard_map/ppermute | solution.py:15
  (6 other events, 17.1 us)
where the time goes:
time: 442 us; the launch traced here: 435 us
  blocking collectives  288 us (65%)
  matrix products  65.8 us (15%)
  waiting for transfers between devices  39.6 us (9%)
  starting transfers between devices  21.3 us (5%)
  other arithmetic  17.8 us (4%)
    psum x1, blocking collectives, local(): loss_total = lax.psum(jnp.sum(log_total - positive_score), ('row', 'col'))  288 us
    dot_general x24, matrix products, backward_block(): toward = jnp.dot(weights, block_rows, preferred_element_type=jnp.float32)  41.9 us
    ppermute x14, waiting for transfers between devices, from_behind(): return lax.ppermute(block, axis, route)  39.6 us
    ppermute x14, starting transfers between devices, from_behind(): return lax.ppermute(block, axis, route)  21.3 us
    dot_general x24, matrix products, block_scores(): lax.dot_general(query_rows, block_rows, (((1,), (1,)), ((), ())), preferr...  12.6 us
    dot_general x24, matrix products, backward_block(): lax.dot_general(weights, query_rows, (((0,), (0,)), ((), ())), preferred_...  11.3 us
  transfers between devices with their start and end apart: 14, of which 4 were waited for; matrix products, arithmetic and copies ran while one was open for 15% of the time, Pallas kernels for 0%

commit v1 on v0

v1 whole, which is shorter than its diff:
```python
import functools

import jax
import jax.numpy as jnp
from jax import lax
from jax.experimental import pallas as pl
from jax.experimental.pallas import tpu as pltpu
from jax.sharding import PartitionSpec as P

MESH = pl.DeviceIdType.MESH
BLK = 128
LOWEST = -1e30
F32, BF16, I32 = jnp.float32, jnp.bfloat16, jnp.int32

OWN, SIB, FRONT, BACK, FAR, Y1, Y2, Y3 = range(8)
SEEN_AS = {SIB: SIB, FRONT: BACK, BACK: FRONT, FAR: FAR, Y1: Y3, Y2: Y2, Y3: Y1}
LOSS_BITS = (1, 16, 2, 4, 8)


def nt(a, b):
    return lax.dot_general(a, b, (((1,), (1,)), ((), ())), preferred_element_type=F32)


def tn(a, b):
    return lax.dot_general(a, b, (((0,), (0,)), ((), ())), preferred_element_type=F32)


def kernel(
    n_row, n_col,
    q_hbm, p_hbm, pos_hbm, bm_hbm, ro_hbm,
    loss_ref, gq_ref, gp_ref,
    q, pall, qr, pos, bm, ro, vis, ebuf, wbuf, mrow, run_m, run_l, lt, psc, meta_out, meta_in, lout, lin,
    loc_s, p_ss, p_rs, q_ss, q_rs, m_ss, m_rs, l_ss, l_rs,
):
    nq, width = q.shape
    np_ = pall.shape[1]
    blocks = np_ // BLK
    scale = width ** (-0.5)
    hq, hp = nq // 2, np_ // 2
    r, c = lax.axis_index("row"), lax.axis_index("col")
    odd = lax.rem(r, 2)
    s = 1 - 2 * odd

    def at_row(o):
        return {"row": lax.rem(r + o + n_row, n_row), "col": c}

    def at_col(o):
        return {"row": r, "col": lax.rem(c + o + n_col, n_col)}

    where = {
        SIB: at_row(s), FRONT: at_row(2 * s), BACK: at_row(-2 * s), FAR: at_row(-s),
        Y1: at_col(-1), Y2: at_col(-2), Y3: at_col(1),
    }
    partner = {
        b: {"row": r + b - 2 * b * lax.rem(lax.div(r, b), 2), "col": c} for b in LOSS_BITS
    }

    barrier = pltpu.get_barrier_semaphore()
    greeted = list(where.values()) + [partner[b] for b in (4, 8, 16)]
    for d in greeted:
        pl.semaphore_signal(barrier, inc=1, device_id=d, device_id_type=MESH)

    loads = [
        pltpu.make_async_copy(src, dst, loc_s.at[i])
        for i, (src, dst) in enumerate(
            ((q_hbm, q), (p_hbm, pall.at[OWN]), (bm_hbm, bm), (ro_hbm, ro), (pos_hbm, pos))
        )
    ]
    for cp in loads:
        cp.start()
    pl.semaphore_wait(barrier, len(greeted))

    class Sender:
        def __init__(self, ss, rs, land):
            self.ss, self.rs, self.land, self.n, self.sent = ss, rs, land, 0, []

        def __call__(self, src, slot, to, first, rows, mark):
            cp = pltpu.make_async_remote_copy(
                src_ref=src.at[pl.ds(first, rows)],
                dst_ref=self.land(slot).at[pl.ds(first, rows)],
                send_sem=self.ss.at[self.n],
                recv_sem=self.rs.at[slot, mark],
                device_id=where[to],
                device_id_type=MESH,
            )
            self.n += 1
            self.sent.append(cp)
            cp.start()
            return cp

    send_p = Sender(p_ss, p_rs, lambda k: pall.at[k])
    send_q = Sender(q_ss, q_rs, lambda k: qr.at[k - 1])

    pa0 = send_p(p_hbm, Y1, Y3, 0, hp, 0)
    pb1 = send_p(p_hbm, Y3, Y1, hp, hp, 1)
    p_front = send_p(p_hbm, BACK, FRONT, 0, np_, 0)
    p_back = send_p(p_hbm, FRONT, BACK, 0, np_, 0)
    p_sib = send_p(p_hbm, SIB, SIB, 0, np_, 0)
    pa1 = send_p(p_hbm, Y1, Y3, hp, hp, 1)
    pb0 = send_p(p_hbm, Y3, Y1, 0, hp, 0)
    q_sib = send_q(q_hbm, SIB, SIB, 0, nq, 0)
    q_front = [send_q(q_hbm, BACK, FRONT, 0, hq, 0)]
    q_back = [send_q(q_hbm, FRONT, BACK, 0, hq, 0)]

    for cp in loads:
        cp.wait()
    row_i = lax.broadcasted_iota(I32, (64, 1), 0)
    slot_i, block_i = lax.shift_right_logical(row_i, 3), lax.bitwise_and(row_i, 7)
    up = jnp.where(odd == 0, jnp.int32(1), jnp.int32(0))
    group = jnp.where(
        slot_i == SIB, 2 + up,
        jnp.where(slot_i == FRONT, 1 + 3 * up, jnp.where(slot_i == BACK, 4 - 3 * up, jnp.where(slot_i == FAR, 3 - up, 0))),
    )
    nb = bm.shape[1]
    wanted = jnp.where((slot_i <= FAR) & (block_i < blocks), group * blocks + block_i, -1)
    pick = jnp.where(lax.broadcasted_iota(I32, (64, nb), 1) == wanted, 1.0, 0.0).astype(BF16)
    seen = nt(pick, bm[...].astype(F32).astype(BF16))
    nr = ro.shape[1]
    pick_r = jnp.where(lax.broadcasted_iota(I32, (64, nr), 1) == slot_i - Y1, 1.0, 0.0).astype(BF16)
    listed = nt(pick_r, ro[...].astype(F32).astype(BF16))
    in_roster = jnp.where(jnp.abs(listed - block_i.astype(F32)) < 0.5, 1.0, 0.0)
    seen = jnp.where(slot_i >= Y1, in_roster, seen)
    pos_row = pos[...]
    own_block = jnp.where((slot_i == OWN) & (lax.shift_right_logical(pos_row, 7) == block_i), 1.0, 0.0)
    seen = jnp.maximum(seen, own_block)
    for k in range(8):
        vis[k] = seen[8 * k : 8 * k + 8]

    run_m[...] = jnp.full(run_m.shape, LOWEST, F32)
    run_l[...] = jnp.zeros(run_l.shape, F32)

    def forward(k):
        @pl.loop(0, 2)
        def _(h):
            cols = pl.ds(pl.multiple_of(h * hq, hq), hq)
            sc = nt(pall[k], q[cols, :]) * scale
            v = vis[k, :, cols]
            m_old = run_m[0:1, cols]
            m_new = m_old
            for b in range(blocks):
                top = jnp.max(sc[b * BLK : (b + 1) * BLK], axis=0, keepdims=True)
                m_new = jnp.maximum(m_new, jnp.where(v[b : b + 1] > 0.5, top, LOWEST))
            total = run_l[0:1, cols] * jnp.exp(m_old - m_new)
            for b in range(blocks):
                bias = jnp.where(v[b : b + 1] > 0.5, -m_new, LOWEST)
                e = jnp.exp(sc[b * BLK : (b + 1) * BLK] + bias)
                total = total + jnp.sum(e, axis=0, keepdims=True)
                ebuf[k, b * BLK : (b + 1) * BLK, cols] = e
            if k == OWN:
                target = lax.broadcasted_iota(I32, (np_, hq), 0) == pos[0:1, cols]
                psc[0:1, cols] = jnp.sum(jnp.where(target, sc, 0.0), axis=0, keepdims=True)
            run_m[0:1, cols] = m_new
            run_l[0:1, cols] = total
            mrow[k, 0:1, cols] = m_new

    forward(OWN)
    p_sib.wait_recv()
    forward(SIB)
    pa0.wait_recv()
    ra = send_p(pall.at[Y1], Y2, Y3, 0, hp, 0)
    pb1.wait_recv()
    rb = send_p(pall.at[Y3], Y2, Y1, hp, hp, 1)
    p_back.wait_recv()
    p_far = send_p(pall.at[FRONT], FAR, SIB, 0, np_, 0)
    p_front.wait_recv()
    pa1.wait_recv()
    pb0.wait_recv()
    qa = [send_q(q_hbm, Y1, Y3, 0, hq, 0)]
    qb = [send_q(q_hbm, Y3, Y1, hq, hq, 1)]
    forward(FRONT)
    forward(BACK)
    forward(Y1)
    forward(Y3)
    p_far.wait_recv()
    forward(FAR)
    ra.wait_recv()
    rb.wait_recv()
    forward(Y2)

    lt[0:1] = run_m[0:1] + jnp.log(run_l[0:1])
    own_loss = jnp.sum(lt[0:1] - psc[0:1], axis=1, keepdims=True)
    metas = {}
    for k in (Y1, Y3, FRONT, BACK, SIB, FAR, Y2):
        rows = jnp.where(vis[k] > 0.5, -lt[0:1], LOWEST)
        last = lax.broadcasted_iota(I32, rows.shape, 0) == 7
        meta_out[k] = jnp.where(last, own_loss, rows)
        seen_as = SEEN_AS[k]
        cp = pltpu.make_async_remote_copy(
            src_ref=meta_out.at[k], dst_ref=meta_in.at[seen_as],
            send_sem=m_ss.at[k], recv_sem=m_rs.at[seen_as],
            device_id=where[k], device_id_type=MESH,
        )
        cp.start()
        metas[seen_as] = cp
    q_front.append(send_q(q_hbm, BACK, FRONT, hq, hq, 1))
    q_back.append(send_q(q_hbm, FRONT, BACK, hq, hq, 1))
    qa.append(send_q(q_hbm, Y1, Y3, hq, hq, 1))
    qb.append(send_q(q_hbm, Y3, Y1, 0, hq, 0))
    q_back[0].wait_recv()
    q_far = [send_q(qr.at[FRONT - 1], FAR, SIB, 0, hq, 0)]

    for k in range(8):
        @pl.loop(0, 2)
        def _(h):
            cols = pl.ds(pl.multiple_of(h * hq, hq), hq)
            factor = jnp.exp(mrow[k, 0:1, cols] - lt[0:1, cols])
            w = ebuf[k, :, cols] * factor
            if k == OWN:
                target = lax.broadcasted_iota(I32, (np_, hq), 0) == pos[0:1, cols]
                w = w - jnp.where(target, 1.0, 0.0)
            wbuf[k * np_ : (k + 1) * np_, cols] = w.astype(BF16)

    gp_ref[...] = jnp.dot(wbuf[0:np_, :], q[...], preferred_element_type=F32) * scale

    @pl.loop(0, 2)
    def _(h):
        cols = pl.ds(pl.multiple_of(h * hq, hq), hq)
        total = tn(wbuf[0:np_, cols], pall[0])
        for k in range(1, 8):
            total = total + tn(wbuf[k * np_ : (k + 1) * np_, cols], pall[k])
        gq_ref[cols, :] = total * scale

    def backward(k, first, rows):
        span = pl.ds(first, rows)
        sc = nt(pall[OWN], qr[k - 1, span, :]) * scale
        parts = []
        for b in range(blocks):
            parts.append(jnp.exp(sc[b * BLK : (b + 1) * BLK] + meta_in[k, b : b + 1, span]).astype(BF16))
        w = jnp.concatenate(parts, axis=0)
        gp_ref[...] += jnp.dot(w, qr[k - 1, span, :], preferred_element_type=F32) * scale

    loss_steps = []

    def loss_send(i, value):
        lout[i] = value
        cp = pltpu.make_async_remote_copy(
            src_ref=lout.at[i], dst_ref=lin.at[i], send_sem=l_ss.at[i], recv_sem=l_rs.at[i],
            device_id=partner[LOSS_BITS[i]], device_id_type=MESH,
        )
        cp.start()
        loss_steps.append(cp)

    def loss_next(i):
        loss_steps[i].wait_recv()
        value = lout[i] + lin[i]
        if i + 1 < len(LOSS_BITS):
            loss_send(i + 1, value)
        else:
            loss_ref[...] = value * (1.0 / (nq * n_row * n_col))

    metas[SIB].wait_recv()
    q_sib.wait_recv()
    backward(SIB, 0, hq)
    backward(SIB, hq, hq)
    metas[FRONT].wait_recv()
    backward(FRONT, 0, hq)
    metas[BACK].wait_recv()
    q_front[0].wait_recv()
    backward(BACK, 0, hq)
    metas[FAR].wait_recv()
    q_far[0].wait_recv()
    backward(FAR, 0, hq)

    qa[0].wait_recv()
    ra2 = [send_q(qr.at[Y1 - 1], Y2, Y3, i * hq // 2, hq // 2, i) for i in range(2)]
    qb[0].wait_recv()
    rb2 = [send_q(qr.at[Y3 - 1], Y2, Y1, hq + i * hq // 2, hq // 2, 2 + i) for i in range(2)]
    metas[Y1].wait_recv()
    metas[Y3].wait_recv()
    metas[Y2].wait_recv()
    spread = lax.broadcasted_iota(I32, (8, 128), 0) >= 0
    loss_at = lambda k: meta_in[k, 7:8, 0:128]
    near = loss_at(Y1) + loss_at(Y3)
    mine = meta_out[Y1, 7:8, 0:128] + loss_at(Y2)
    loss_send(0, jnp.where(spread, near + mine, 0.0))
    backward(Y1, 0, hq)
    backward(Y3, hq, hq)
    loss_next(0)
    q_back[1].wait_recv()
    q_far.append(send_q(qr.at[FRONT - 1], FAR, SIB, hq, hq, 1))
    backward(FRONT, hq, hq)
    q_front[1].wait_recv()
    backward(BACK, hq, hq)
    loss_next(1)
    q_far[1].wait_recv()
    backward(FAR, hq, hq)
    loss_next(2)
    qa[1].wait_recv()
    backward(Y1, hq, hq)
    loss_next(3)
    qb[1].wait_recv()
    backward(Y3, 0, hq)
    loss_next(4)
    for i in range(2):
        ra2[i].wait_recv()
        backward(Y2, i * hq // 2, hq // 2)
        rb2[i].wait_recv()
        backward(Y2, hq + i * hq // 2, hq // 2)

    for cp in send_p.sent + send_q.sent + list(metas.values()) + loss_steps:
        cp.wait_send()


def local(n_row, n_col, queries, passages, positive, block_mask, roster):
    nq, width = queries.shape
    np_ = passages.shape[0]
    nb, nr = block_mask.shape[1], roster.shape[1]
    anywhere = pl.BlockSpec(memory_space=pl.ANY)
    inside = pl.BlockSpec(memory_space=pltpu.VMEM)
    dma = pltpu.SemaphoreType.DMA
    loss, gq, gp = pl.pallas_call(
        functools.partial(kernel, n_row, n_col),
        out_shape=(
            jax.ShapeDtypeStruct((8, 128), F32),
            jax.ShapeDtypeStruct((nq, width), F32),
            jax.ShapeDtypeStruct((np_, width), F32),
        ),
        in_specs=[anywhere] * 5,
        out_specs=(inside,) * 3,
        scratch_shapes=[
            pltpu.VMEM((nq, width), BF16),
            pltpu.VMEM((8, np_, width), BF16),
            pltpu.VMEM((7, nq, width), BF16),
            pltpu.VMEM((1, nq), I32),
            pltpu.VMEM((nq, nb), I32),
            pltpu.VMEM((nq, nr), I32),
            pltpu.VMEM((8, 8, nq), F32),
            pltpu.VMEM((8, np_, nq), F32),
            pltpu.VMEM((8 * np_, nq), BF16),
            pltpu.VMEM((8, 8, nq), F32),
            pltpu.VMEM((8, nq), F32),
            pltpu.VMEM((8, nq), F32),
            pltpu.VMEM((8, nq), F32),
            pltpu.VMEM((8, nq), F32),
            pltpu.VMEM((8, 8, nq), F32),
            pltpu.VMEM((8, 8, nq), F32),
            pltpu.VMEM((5, 8, 128), F32),
            pltpu.VMEM((5, 8, 128), F32),
            dma((5,)),
            dma((10,)),
            dma((8, 2)),
            dma((16,)),
            dma((8, 4)),
            dma((8,)),
            dma((8,)),
            dma((5,)),
            dma((5,)),
        ],
        compiler_params=pltpu.CompilerParams(
            collective_id=0, has_side_effects=True, vmem_limit_bytes=48 * 2**20
        ),
        cost_estimate=pl.CostEstimate(flops=10**10, bytes_accessed=10**7, transcendentals=4 * 10**6),
    )(queries, passages, positive.reshape(1, nq), block_mask, roster)
    return loss[0, 0:1], gq, gp


def solution(mesh):
    whole = P(("rep", "row", "col"), None)
    return jax.shard_map(
        functools.partial(local, mesh.shape["row"], mesh.shape["col"]),
        mesh=mesh,
        in_specs=(whole, whole, P(("rep", "row", "col")), whole, whole),
        out_specs=(P("rep"), whole, whole),
        check_vma=False,
    )
```

time: 442 us -> 66.5 us (0.15); the launches traced: 435 us -> 66 us
  blocking collectives: 288 us -> 0 us
  matrix products: 65.8 us -> 0 us
  Pallas kernels: 0 us -> 58.1 us
  waiting for transfers between devices: 39.6 us -> 0 us
  starting transfers between devices: 21.3 us -> 0 us
  other arithmetic: 17.8 us -> 0 us
  local copies, waits for them, and re-layouts: 0.07 us -> 7.27 us
    psum x1 -> x0, blocking collectives: 288 us -> none  [local(): loss_total = lax.psum(jnp.sum(log_total - positive_score), ('row', 'col'))]
    dot_general x72 -> x0, matrix products: 65.8 us -> none  [the longest x24 41.9 us: backward_block(): toward = jnp.dot(weights, block_rows, preferred_element_type=jnp.float32)]
    pallas_call x0 -> x1, Pallas kernels: none -> 58.1 us  [local(): pl.pallas_call(functools.partial(kernel, n_row, n_col), out_shape=(jax.Sh...]
    ppermute x14 -> x0, waiting for transfers between devices: 39.6 us -> none  [from_behind(): return lax.ppermute(block, axis, route)]
    ppermute x14 -> x0, starting transfers between devices: 21.3 us -> none  [from_behind(): return lax.ppermute(block, axis, route)]
    add x5 -> x0, other arithmetic: 8.37 us -> none  [the longest x1 4.27 us: local(): grad_passages = own_gradient + returned + arrived]
    unnamed x32 -> x10, local copies, waits for them, and re-layouts: 0.07 us -> 6.76 us
    concatenate x5 -> x0, other arithmetic: 4.51 us -> none  [cell_backward(): return (toward_sum, jnp.concatenate(pieces, axis=0))]
  transfers between devices with their start and end apart: 14 -> 0, of which waited for: 4 -> 0; matrix products, arithmetic and copies ran while one was open for 15% -> 0% of each run, Pallas kernels for 0% -> 0%
where the time goes in v1:
time: 66.5 us; the launch traced here: 66 us
  Pallas kernels  58.1 us (87%)
  local copies, waits for them, and re-layouts  7.27 us (11%)
  between operations  0.67 us (1%)
    pallas_call x1, Pallas kernels, local(): pl.pallas_call(functools.partial(kernel, n_row, n_col), out_shape=(jax.Sh...  58.1 us
    unnamed x10, local copies, waits for them, and re-layouts  6.76 us

profile of v1, /device:TPU:1, one launch (start us, length us, event | category | flops | bytes accessed | tf_op | source)
XLA Modules:
  0.0 66.0 jit_solution(935678855651617122)
XLA Ops:
  0.6 0.9 %copy.8.bm_hbm = s32[512,15]{1,0:T(8,128)S(1)} copy(s32[512,15]{0,1:T(8,128)} %param.8) | data formatting | bytes 61440 | tf_op args[3]
  1.5 0.8 %copy.9.ro_hbm = s32[512,3]{1,0:T(8,128)S(1)} copy(s32[512,3]{0,1:T(4,128)} %param.9) | data formatting | bytes 12288 | tf_op args[4]
  2.4 0.0 copy-start
  2.4 1.1 %copy-done = bf16[512,768]{1,0:T(8,128)(2,1)S(1)} copy-done((bf16[512,768]{1,0:T(8,128)(2,1)S(1)}, bf16[512,768]{1,0:T(8,128)(2,1)}, u32[]{:S(2)}) %copy-start) | copy-done | bytes 786456
  3.5 0.0 copy-start.1
  3.5 1.1 %copy-done.1 = bf16[384,768]{1,0:T(8,128)(2,1)S(1)} copy-done((bf16[384,768]{1,0:T(8,128)(2,1)S(1)}, bf16[384,768]{1,0:T(8,128)(2,1)}, u32[]{:S(2)}) %copy-start.1) | copy-done | bytes 589848
  4.6 0.0 copy-start.2
  4.6 0.7 %copy-done.2 = s32[512]{0:T(512)S(1)} copy-done((s32[512]{0:T(512)S(1)}, s32[512]{0:T(512)}, u32[]{:S(2)}) %copy-start.2) | copy-done | bytes 2072
  5.3 58.1 %shard_map.76 = (f32[8,128]{1,0:T(8,128)S(1)}, f32[512,768]{1,0:T(8,128)S(1)}, f32[384,768]{1,0:T(8,128)S(1)}) custom-call(bf16[512,768]{1,0:T(8,128)(2,1)S(1)} %copy-done, bf16[384,768]{1,0:T(8,128)(2,1)S(1)} %copy-done.1, s32[1,512]{1,0:T(1,128)S(1)} %bitcast.2, s32[512,15]{1,0:T(8,128)S(1)} %copy.8.bm_hbm, s32[512,3]{1,0:T(8,128)S(1)} %copy.9.ro_hbm), custom_call_target="tpu_custom_call" | custom-call | flops 10000000000 | bytes 10000000 | tf_op jit(solution)/shard_map/pallas_call | solution.py:311
  63.3 0.5 slice.3
  63.8 1.1 %copy.12 = f32[512,768]{1,0:T(8,128)} copy(f32[512,768]{1,0:T(8,128)S(1)} %get-tuple-element.13) | data formatting | bytes 3145728
  65.0 1.0 %copy.13 = f32[384,768]{1,0:T(8,128)} copy(f32[384,768]{1,0:T(8,128)S(1)} %get-tuple-element.14) | data formatting | bytes 2359296
Async XLA Ops:
  2.4 1.1 %copy-start = (bf16[512,768]{1,0:T(8,128)(2,1)S(1)}, bf16[512,768]{1,0:T(8,128)(2,1)}, u32[]{:S(2)}) copy-start(bf16[512,768]{1,0:T(8,128)(2,1)} %q_hbm.1) | copy-start | bytes 2359300
  3.5 1.1 %copy-start.1 = (bf16[384,768]{1,0:T(8,128)(2,1)S(1)}, bf16[384,768]{1,0:T(8,128)(2,1)}, u32[]{:S(2)}) copy-start(bf16[384,768]{1,0:T(8,128)(2,1)} %p_hbm.1) | copy-start | bytes 1769476
  4.6 0.7 %copy-start.2 = (s32[512]{0:T(512)S(1)}, s32[512]{0:T(512)}, u32[]{:S(2)}) copy-start(s32[512]{0:T(512)} %param.7) | copy-start | bytes 6148

commit v2 on v1

--- a/solution.py
+++ b/solution.py
@@ -111,13 +111,13 @@
         slot_i == SIB, 2 + up,
         jnp.where(slot_i == FRONT, 1 + 3 * up, jnp.where(slot_i == BACK, 4 - 3 * up, jnp.where(slot_i == FAR, 3 - up, 0))),
     )
-    nb = bm.shape[1]
+    nb = bm.shape[0]
     wanted = jnp.where((slot_i <= FAR) & (block_i < blocks), group * blocks + block_i, -1)
     pick = jnp.where(lax.broadcasted_iota(I32, (64, nb), 1) == wanted, 1.0, 0.0).astype(BF16)
-    seen = nt(pick, bm[...].astype(F32).astype(BF16))
-    nr = ro.shape[1]
+    seen = jnp.dot(pick, bm[...].astype(F32).astype(BF16), preferred_element_type=F32)
+    nr = ro.shape[0]
     pick_r = jnp.where(lax.broadcasted_iota(I32, (64, nr), 1) == slot_i - Y1, 1.0, 0.0).astype(BF16)
-    listed = nt(pick_r, ro[...].astype(F32).astype(BF16))
+    listed = jnp.dot(pick_r, ro[...].astype(F32).astype(BF16), preferred_element_type=F32)
     in_roster = jnp.where(jnp.abs(listed - block_i.astype(F32)) < 0.5, 1.0, 0.0)
     seen = jnp.where(slot_i >= Y1, in_roster, seen)
     pos_row = pos[...]
@@ -301,13 +301,23 @@
         cp.wait_send()
 
 
+def finish(loss, gq, gp, loss_out, gq_out, gp_out, sems):
+    copies = [pltpu.make_async_copy(gq, gq_out, sems.at[0]), pltpu.make_async_copy(gp, gp_out, sems.at[1])]
+    for cp in copies:
+        cp.start()
+    loss_out[0] = loss[0, 0]
+    for cp in copies:
+        cp.wait()
+
+
 def local(n_row, n_col, queries, passages, positive, block_mask, roster):
     nq, width = queries.shape
     np_ = passages.shape[0]
     nb, nr = block_mask.shape[1], roster.shape[1]
-    anywhere = pl.BlockSpec(memory_space=pl.ANY)
+    anywhere = pl.BlockSpec(memory_space=pltpu.HBM)
     inside = pl.BlockSpec(memory_space=pltpu.VMEM)
     dma = pltpu.SemaphoreType.DMA
+    operands = (queries, passages, positive.reshape(1, nq), block_mask.T, roster.T)
     loss, gq, gp = pl.pallas_call(
         functools.partial(kernel, n_row, n_col),
         out_shape=(
@@ -322,8 +332,8 @@
             pltpu.VMEM((8, np_, width), BF16),
             pltpu.VMEM((7, nq, width), BF16),
             pltpu.VMEM((1, nq), I32),
-            pltpu.VMEM((nq, nb), I32),
-            pltpu.VMEM((nq, nr), I32),
+            pltpu.VMEM((nb, nq), I32),
+            pltpu.VMEM((nr, nq), I32),
             pltpu.VMEM((8, 8, nq), F32),
             pltpu.VMEM((8, np_, nq), F32),
             pltpu.VMEM((8 * np_, nq), BF16),
@@ -350,8 +360,19 @@
             collective_id=0, has_side_effects=True, vmem_limit_bytes=48 * 2**20
         ),
         cost_estimate=pl.CostEstimate(flops=10**10, bytes_accessed=10**7, transcendentals=4 * 10**6),
-    )(queries, passages, positive.reshape(1, nq), block_mask, roster)
-    return loss[0, 0:1], gq, gp
+    )(*(pltpu.with_memory_space_constraint(a, pltpu.HBM) for a in operands))
+    return pl.pallas_call(
+        finish,
+        out_shape=(
+            jax.ShapeDtypeStruct((1,), F32),
+            jax.ShapeDtypeStruct((nq, width), F32),
+            jax.ShapeDtypeStruct((np_, width), F32),
+        ),
+        in_specs=[inside] * 3,
+        out_specs=(pl.BlockSpec(memory_space=pltpu.SMEM), anywhere, anywhere),
+        scratch_shapes=[dma((2,))],
+        compiler_params=pltpu.CompilerParams(vmem_limit_bytes=4 * 2**20),
+    )(loss, gq, gp)
 
 
 def solution(mesh):

time: 66.5 us -> 61.7 us (0.928)
  local copies, waits for them, and re-layouts: 7.27 us -> 0 us
  Pallas kernels: 58.1 us -> 60.6 us
    unnamed x10 -> x0, local copies, waits for them, and re-layouts: 6.76 us -> none
    pallas_call x0 -> x1, Pallas kernels: none -> 2.07 us  [local(): pl.pallas_call(finish, out_shape=(jax.ShapeDtypeStruct((1,), F32), jax.Sh...]
where the time goes in v2:
time: 61.7 us; the launch traced here: 61.4 us
  Pallas kernels  60.6 us (98%)
  between operations  0.8 us (1%)
    pallas_call x1, Pallas kernels, local(): pl.pallas_call(functools.partial(kernel, n_row, n_col), out_shape=(jax.Sh...  58.5 us
    pallas_call x1, Pallas kernels, local(): pl.pallas_call(finish, out_shape=(jax.ShapeDtypeStruct((1,), F32), jax.Sh...  2.07 us

profile of v2, /device:TPU:1, one launch (start us, length us, event | category | flops | bytes accessed | tf_op | source)
XLA Modules:
  0.0 61.4 jit_solution(2499132887546531136)
XLA Ops:
  0.6 58.5 %shard_map.76 = (f32[8,128]{1,0:T(8,128)S(1)}, f32[512,768]{1,0:T(8,128)S(1)}, f32[384,768]{1,0:T(8,128)S(1)}) custom-call(bf16[512,768]{1,0:T(8,128)(2,1)} %q_hbm.1, bf16[384,768]{1,0:T(8,128)(2,1)} %p_hbm.1, s32[1,512]{1,0:T(1,128)} %bitcast.5, s32[15,512]{1,0:T(8,128)} %bitcast.3, s32[3,512]{1,0:T(4,128)} %bitcast.4), custom_call_target="tpu_custom_call" | custom-call | flops 10000000000 | bytes 10000000 | tf_op jit(solution)/shard_map/pallas_call | solution.py:321
  59.2 2.1 %shard_map.77 = (f32[1]{0:T(128)}, f32[512,768]{1,0:T(8,128)}, f32[384,768]{1,0:T(8,128)}) custom-call(f32[8,128]{1,0:T(8,128)S(1)} %get-tuple-element.6.loss, f32[512,768]{1,0:T(8,128)S(1)} %get-tuple-element.7.gq, f32[384,768]{1,0:T(8,128)S(1)} %get-tuple-element.8.gp), custom_call_target="tpu_custom_call" | custom-call | tf_op jit(solution)/shard_map/pallas_call | solution.py:364

commit v3 on v2

--- a/solution.py
+++ b/solution.py
@@ -14,7 +14,6 @@
 
 OWN, SIB, FRONT, BACK, FAR, Y1, Y2, Y3 = range(8)
 SEEN_AS = {SIB: SIB, FRONT: BACK, BACK: FRONT, FAR: FAR, Y1: Y3, Y2: Y2, Y3: Y1}
-LOSS_BITS = (1, 16, 2, 4, 8)
 
 
 def nt(a, b):
@@ -26,11 +25,11 @@
 
 
 def kernel(
-    n_row, n_col,
+    n_row, n_col, n_z,
     q_hbm, p_hbm, pos_hbm, bm_hbm, ro_hbm,
     loss_ref, gq_ref, gp_ref,
-    q, pall, qr, pos, bm, ro, vis, ebuf, wbuf, mrow, run_m, run_l, lt, psc, meta_out, meta_in, lout, lin,
-    loc_s, p_ss, p_rs, q_ss, q_rs, m_ss, m_rs, l_ss, l_rs,
+    q, pall, qr, pos, bm, ro, vis, ebuf, wbuf, mrow, run_m, run_l, lt, psc, meta_out, meta_in, zin, xin,
+    loc_s, p_ss, p_rs, q_ss, q_rs, m_ss, m_rs, z_ss, z_rs, x_ss, x_rs, y_in, z_in,
 ):
     nq, width = q.shape
     np_ = pall.shape[1]
@@ -51,14 +50,28 @@
         SIB: at_row(s), FRONT: at_row(2 * s), BACK: at_row(-2 * s), FAR: at_row(-s),
         Y1: at_col(-1), Y2: at_col(-2), Y3: at_col(1),
     }
-    partner = {
-        b: {"row": r + b - 2 * b * lax.rem(lax.div(r, b), 2), "col": c} for b in LOSS_BITS
-    }
+    z = lax.rem(lax.div(r, 2), n_z)
+    side = lax.div(r, 2 * n_z)
+    along_z = {i: {"row": side * 2 * n_z + 2 * lax.rem(z + i, n_z) + odd, "col": c} for i in range(1, n_z)}
+    over_x = (1 - side) * 2 * n_z + 2 * z
+    same_z = {1: where[SIB], 2: {"row": over_x + odd, "col": c}, 3: {"row": over_x + 1 - odd, "col": c}}
 
     barrier = pltpu.get_barrier_semaphore()
-    greeted = list(where.values()) + [partner[b] for b in (4, 8, 16)]
-    for d in greeted:
-        pl.semaphore_signal(barrier, inc=1, device_id=d, device_id_type=MESH)
+    chip = r - odd
+    even_core, odd_core = {"row": chip, "col": c}, {"row": chip + 1, "col": c}
+    for o in range(1, n_col):
+        pl.semaphore_signal(
+            barrier, inc=1, device_id={"row": chip, "col": lax.rem(c + o, n_col)}, device_id_type=MESH
+        )
+
+    @pl.when(odd == 1)
+    def _():
+        pl.semaphore_signal(barrier, inc=1, device_id=even_core, device_id_type=MESH)
+
+    chips = [lax.rem(chip + 2, n_row), lax.rem(chip + n_row - 2, n_row), over_x]
+    chips += [to["row"] - odd for to in along_z.values()]
+    for there in chips:
+        pl.semaphore_signal(barrier, inc=1, device_id={"row": there + 1, "col": c}, device_id_type=MESH)
 
     loads = [
         pltpu.make_async_copy(src, dst, loc_s.at[i])
@@ -68,7 +81,15 @@
     ]
     for cp in loads:
         cp.start()
-    pl.semaphore_wait(barrier, len(greeted))
+
+    @pl.when(odd == 0)
+    def _():
+        pl.semaphore_wait(barrier, 2 * (n_col - 1) + 1)
+        pl.semaphore_signal(y_in, inc=1, device_id=odd_core, device_id_type=MESH)
+
+    @pl.when(odd == 1)
+    def _():
+        pl.semaphore_wait(y_in, 1)
 
     class Sender:
         def __init__(self, ss, rs, land):
@@ -93,14 +114,25 @@
 
     pa0 = send_p(p_hbm, Y1, Y3, 0, hp, 0)
     pb1 = send_p(p_hbm, Y3, Y1, hp, hp, 1)
+    pa1 = send_p(p_hbm, Y1, Y3, hp, hp, 1)
+    pb0 = send_p(p_hbm, Y3, Y1, 0, hp, 0)
+    p_sib = send_p(p_hbm, SIB, SIB, 0, np_, 0)
+    q_sib = send_q(q_hbm, SIB, SIB, 0, nq, 0)
+
+    @pl.when(odd == 1)
+    def _():
+        pl.semaphore_wait(barrier, 2 * len(chips))
+        pl.semaphore_signal(z_in, inc=1, device_id=even_core, device_id_type=MESH)
+
+    @pl.when(odd == 0)
+    def _():
+        pl.semaphore_wait(z_in, 1)
+
     p_front = send_p(p_hbm, BACK, FRONT, 0, np_, 0)
     p_back = send_p(p_hbm, FRONT, BACK, 0, np_, 0)
-    p_sib = send_p(p_hbm, SIB, SIB, 0, np_, 0)
-    pa1 = send_p(p_hbm, Y1, Y3, hp, hp, 1)
-    pb0 = send_p(p_hbm, Y3, Y1, 0, hp, 0)
-    q_sib = send_q(q_hbm, SIB, SIB, 0, nq, 0)
-    q_front = [send_q(q_hbm, BACK, FRONT, 0, hq, 0)]
-    q_back = [send_q(q_hbm, FRONT, BACK, 0, hq, 0)]
+    qz = nq * 5 // 8
+    q_front = [send_q(q_hbm, BACK, FRONT, 0, qz, 0)]
+    q_back = [send_q(q_hbm, FRONT, BACK, 0, qz, 0)]
 
     for cp in loads:
         cp.wait()
@@ -160,22 +192,23 @@
     ra = send_p(pall.at[Y1], Y2, Y3, 0, hp, 0)
     pb1.wait_recv()
     rb = send_p(pall.at[Y3], Y2, Y1, hp, hp, 1)
+    pa1.wait_recv()
+    pb0.wait_recv()
+    qe, qs = nq // 4, nq // 8
+    qa = [send_q(q_hbm, Y1, Y3, 0, qe, 0)]
+    qb = [send_q(q_hbm, Y3, Y1, nq - qe, qe, 0)]
+    forward(Y1)
+    forward(Y3)
     p_back.wait_recv()
     p_far = send_p(pall.at[FRONT], FAR, SIB, 0, np_, 0)
     p_front.wait_recv()
-    pa1.wait_recv()
-    pb0.wait_recv()
-    qa = [send_q(q_hbm, Y1, Y3, 0, hq, 0)]
-    qb = [send_q(q_hbm, Y3, Y1, hq, hq, 1)]
     forward(FRONT)
     forward(BACK)
-    forward(Y1)
-    forward(Y3)
-    p_far.wait_recv()
-    forward(FAR)
     ra.wait_recv()
     rb.wait_recv()
     forward(Y2)
+    p_far.wait_recv()
+    forward(FAR)
 
     lt[0:1] = run_m[0:1] + jnp.log(run_l[0:1])
     own_loss = jnp.sum(lt[0:1] - psc[0:1], axis=1, keepdims=True)
@@ -192,12 +225,10 @@
         )
         cp.start()
         metas[seen_as] = cp
-    q_front.append(send_q(q_hbm, BACK, FRONT, hq, hq, 1))
-    q_back.append(send_q(q_hbm, FRONT, BACK, hq, hq, 1))
-    qa.append(send_q(q_hbm, Y1, Y3, hq, hq, 1))
-    qb.append(send_q(q_hbm, Y3, Y1, 0, hq, 0))
+    qa += [send_q(q_hbm, Y1, Y3, qe, qe, 1), send_q(q_hbm, Y1, Y3, hq, hq, 2)]
+    qb += [send_q(q_hbm, Y3, Y1, hq, qe, 1), send_q(q_hbm, Y3, Y1, 0, hq, 2)]
     q_back[0].wait_recv()
-    q_far = [send_q(qr.at[FRONT - 1], FAR, SIB, 0, hq, 0)]
+    q_far = [send_q(qr.at[FRONT - 1], FAR, SIB, 0, qz, 0)]
 
     for k in range(8):
         @pl.loop(0, 2)
@@ -229,29 +260,42 @@
         w = jnp.concatenate(parts, axis=0)
         gp_ref[...] += jnp.dot(w, qr[k - 1, span, :], preferred_element_type=F32) * scale
 
-    loss_steps = []
-
-    def loss_send(i, value):
-        lout[i] = value
-        cp = pltpu.make_async_remote_copy(
-            src_ref=lout.at[i], dst_ref=lin.at[i], send_sem=l_ss.at[i], recv_sem=l_rs.at[i],
-            device_id=partner[LOSS_BITS[i]], device_id_type=MESH,
-        )
-        cp.start()
-        loss_steps.append(cp)
-
-    def loss_next(i):
-        loss_steps[i].wait_recv()
-        value = lout[i] + lin[i]
-        if i + 1 < len(LOSS_BITS):
-            loss_send(i + 1, value)
-        else:
-            loss_ref[...] = value * (1.0 / (nq * n_row * n_col))
-
+    loss_at = lambda k: meta_in[k, 7:8, 0:128]
+    for k in (Y1, Y3, Y2):
+        metas[k].wait_recv()
+    near = loss_at(Y1) + loss_at(Y3)
+    mine = meta_out[Y1, 7:8, 0:128] + loss_at(Y2)
+    zin[0] = jnp.broadcast_to(near + mine, (8, 128))
+
+    def spread(buf, ss, rs, partners):
+        copies = []
+        for i, to in partners.items():
+            cp = pltpu.make_async_remote_copy(
+                src_ref=buf.at[0], dst_ref=buf.at[i], send_sem=ss.at[i], recv_sem=rs.at[i],
+                device_id=to, device_id_type=MESH,
+            )
+            cp.start()
+            copies.append(cp)
+        return copies
+
+    loss_z = spread(zin, z_ss, z_rs, along_z)
+    q_front.append(send_q(q_hbm, BACK, FRONT, qz, nq - qz, 1))
+    q_back.append(send_q(q_hbm, FRONT, BACK, qz, nq - qz, 1))
+
+    qa[0].wait_recv()
+    ra2 = [send_q(qr.at[Y1 - 1], Y2, Y3, 0, qe, 0)]
+    qb[0].wait_recv()
+    rb2 = [send_q(qr.at[Y3 - 1], Y2, Y1, nq - qe, qe, 3)]
     metas[SIB].wait_recv()
     q_sib.wait_recv()
     backward(SIB, 0, hq)
     backward(SIB, hq, hq)
+    qa[1].wait_recv()
+    ra2 += [send_q(qr.at[Y1 - 1], Y2, Y3, qe + i * qs, qs, 1 + i) for i in range(2)]
+    qb[1].wait_recv()
+    rb2 += [send_q(qr.at[Y3 - 1], Y2, Y1, nq - qe - (i + 1) * qs, qs, 4 + i) for i in range(2)]
+    backward(Y1, 0, hq)
+    backward(Y3, hq, hq)
     metas[FRONT].wait_recv()
     backward(FRONT, 0, hq)
     metas[BACK].wait_recv()
@@ -260,44 +304,40 @@
     metas[FAR].wait_recv()
     q_far[0].wait_recv()
     backward(FAR, 0, hq)
-
-    qa[0].wait_recv()
-    ra2 = [send_q(qr.at[Y1 - 1], Y2, Y3, i * hq // 2, hq // 2, i) for i in range(2)]
-    qb[0].wait_recv()
-    rb2 = [send_q(qr.at[Y3 - 1], Y2, Y1, hq + i * hq // 2, hq // 2, 2 + i) for i in range(2)]
-    metas[Y1].wait_recv()
-    metas[Y3].wait_recv()
-    metas[Y2].wait_recv()
-    spread = lax.broadcasted_iota(I32, (8, 128), 0) >= 0
-    loss_at = lambda k: meta_in[k, 7:8, 0:128]
-    near = loss_at(Y1) + loss_at(Y3)
-    mine = meta_out[Y1, 7:8, 0:128] + loss_at(Y2)
-    loss_send(0, jnp.where(spread, near + mine, 0.0))
-    backward(Y1, 0, hq)
-    backward(Y3, hq, hq)
-    loss_next(0)
+    for cp in loss_z:
+        cp.wait_recv()
+    total = zin[z]
+    for i in range(1, n_z):
+        total = total + zin[lax.rem(z + n_z - i, n_z)]
+    xin[0] = total
+    loss_x = spread(xin, x_ss, x_rs, same_z)
     q_back[1].wait_recv()
-    q_far.append(send_q(qr.at[FRONT - 1], FAR, SIB, hq, hq, 1))
+    q_far.append(send_q(qr.at[FRONT - 1], FAR, SIB, qz, nq - qz, 1))
     backward(FRONT, hq, hq)
     q_front[1].wait_recv()
     backward(BACK, hq, hq)
-    loss_next(1)
+    qa[2].wait_recv()
+    backward(Y1, hq, hq)
+    qb[2].wait_recv()
+    backward(Y3, 0, hq)
     q_far[1].wait_recv()
     backward(FAR, hq, hq)
-    loss_next(2)
-    qa[1].wait_recv()
-    backward(Y1, hq, hq)
-    loss_next(3)
-    qb[1].wait_recv()
-    backward(Y3, 0, hq)
-    loss_next(4)
-    for i in range(2):
-        ra2[i].wait_recv()
-        backward(Y2, i * hq // 2, hq // 2)
-        rb2[i].wait_recv()
-        backward(Y2, hq + i * hq // 2, hq // 2)
-
-    for cp in send_p.sent + send_q.sent + list(metas.values()) + loss_steps:
+    ra2[0].wait_recv()
+    backward(Y2, 0, qe)
+    rb2[0].wait_recv()
+    backward(Y2, nq - qe, qe)
+    for cp in loss_x:
+        cp.wait_recv()
+    loss_ref[...] = ((xin[0] + xin[1]) + (xin[2] + xin[3])) * (1.0 / (nq * n_row * n_col))
+    ra2[1].wait_recv()
+    rb2[1].wait_recv()
+    backward(Y2, qe, qs)
+    backward(Y2, nq - qe - qs, qs)
+    ra2[2].wait_recv()
+    rb2[2].wait_recv()
+    backward(Y2, hq - qs, 2 * qs)
+
+    for cp in send_p.sent + send_q.sent + list(metas.values()) + loss_z + loss_x:
         cp.wait_send()
 
 
@@ -313,13 +353,14 @@
 def local(n_row, n_col, queries, passages, positive, block_mask, roster):
     nq, width = queries.shape
     np_ = passages.shape[0]
+    n_z = n_row // 4
     nb, nr = block_mask.shape[1], roster.shape[1]
     anywhere = pl.BlockSpec(memory_space=pltpu.HBM)
     inside = pl.BlockSpec(memory_space=pltpu.VMEM)
     dma = pltpu.SemaphoreType.DMA
     operands = (queries, passages, positive.reshape(1, nq), block_mask.T, roster.T)
     loss, gq, gp = pl.pallas_call(
-        functools.partial(kernel, n_row, n_col),
+        functools.partial(kernel, n_row, n_col, n_z),
         out_shape=(
             jax.ShapeDtypeStruct((8, 128), F32),
             jax.ShapeDtypeStruct((nq, width), F32),
@@ -344,17 +385,21 @@
             pltpu.VMEM((8, nq), F32),
             pltpu.VMEM((8, 8, nq), F32),
             pltpu.VMEM((8, 8, nq), F32),
-            pltpu.VMEM((5, 8, 128), F32),
-            pltpu.VMEM((5, 8, 128), F32),
+            pltpu.VMEM((n_z, 8, 128), F32),
+            pltpu.VMEM((4, 8, 128), F32),
             dma((5,)),
             dma((10,)),
             dma((8, 2)),
-            dma((16,)),
-            dma((8, 4)),
+            dma((19,)),
+            dma((8, 6)),
             dma((8,)),
             dma((8,)),
-            dma((5,)),
-            dma((5,)),
+            dma((n_z,)),
+            dma((n_z,)),
+            dma((4,)),
+            dma((4,)),
+            pltpu.SemaphoreType.REGULAR,
+            pltpu.SemaphoreType.REGULAR,
         ],
         compiler_params=pltpu.CompilerParams(
             collective_id=0, has_side_effects=True, vmem_limit_bytes=48 * 2**20

time: 61.7 us -> 60.7 us (0.984)
  Pallas kernels: 60.6 us -> 59.8 us
    pallas_call x1, Pallas kernels: 58.5 us -> 57.8 us  [local(): pl.pallas_call(functools.partial(kernel, n_row, n_col, n_z), out_shape=(j...]
where the time goes in v3:
time: 60.7 us; the launch traced here: 60.6 us
  Pallas kernels  59.8 us (99%)
  between operations  0.8 us (1%)
    pallas_call x1, Pallas kernels, local(): pl.pallas_call(functools.partial(kernel, n_row, n_col, n_z), out_shape=(j...  57.8 us
    pallas_call x1, Pallas kernels, local(): pl.pallas_call(finish, out_shape=(jax.ShapeDtypeStruct((1,), F32), jax.Sh...  2.07 us

profile of v3, /device:TPU:1, one launch (start us, length us, event | category | flops | bytes accessed | tf_op | source)
XLA Modules:
  0.0 60.6 jit_solution(17780696721001885124)
XLA Ops:
  0.6 57.8 %shard_map.76 = (f32[8,128]{1,0:T(8,128)S(1)}, f32[512,768]{1,0:T(8,128)S(1)}, f32[384,768]{1,0:T(8,128)S(1)}) custom-call(bf16[512,768]{1,0:T(8,128)(2,1)} %q_hbm.1, bf16[384,768]{1,0:T(8,128)(2,1)} %p_hbm.1, s32[1,512]{1,0:T(1,128)} %bitcast.5, s32[15,512]{1,0:T(8,128)} %bitcast.3, s32[3,512]{1,0:T(4,128)} %bitcast.4), custom_call_target="tpu_custom_call" | custom-call | flops 10000000000 | bytes 10000000 | tf_op jit(solution)/shard_map/pallas_call | solution.py:362
  58.4 2.1 %shard_map.77 = (f32[1]{0:T(128)}, f32[512,768]{1,0:T(8,128)}, f32[384,768]{1,0:T(8,128)}) custom-call(f32[8,128]{1,0:T(8,128)S(1)} %get-tuple-element.6.loss, f32[512,768]{1,0:T(8,128)S(1)} %get-tuple-element.7.gq, f32[384,768]{1,0:T(8,128)S(1)} %get-tuple-element.8.gp), custom_call_target="tpu_custom_call" | custom-call | tf_op jit(solution)/shard_map/pallas_call | solution.py:409

commit v4 on v3

--- a/solution.py
+++ b/solution.py
@@ -194,9 +194,9 @@
     rb = send_p(pall.at[Y3], Y2, Y1, hp, hp, 1)
     pa1.wait_recv()
     pb0.wait_recv()
-    qe, qs = nq // 4, nq // 8
-    qa = [send_q(q_hbm, Y1, Y3, 0, qe, 0)]
-    qb = [send_q(q_hbm, Y3, Y1, nq - qe, qe, 0)]
+    qe, qs, q0 = nq // 4, nq // 8, nq * 3 // 8
+    qa = [send_q(q_hbm, Y1, Y3, 0, q0, 0), send_q(q_hbm, Y1, Y3, q0, hq - q0, 1)]
+    qb = [send_q(q_hbm, Y3, Y1, nq - q0, q0, 0), send_q(q_hbm, Y3, Y1, hq, hq - q0, 1)]
     forward(Y1)
     forward(Y3)
     p_back.wait_recv()
@@ -204,16 +204,16 @@
     p_front.wait_recv()
     forward(FRONT)
     forward(BACK)
+    p_far.wait_recv()
+    forward(FAR)
     ra.wait_recv()
     rb.wait_recv()
     forward(Y2)
-    p_far.wait_recv()
-    forward(FAR)
 
     lt[0:1] = run_m[0:1] + jnp.log(run_l[0:1])
     own_loss = jnp.sum(lt[0:1] - psc[0:1], axis=1, keepdims=True)
     metas = {}
-    for k in (Y1, Y3, FRONT, BACK, SIB, FAR, Y2):
+    for k in (Y1, Y3, Y2, FRONT, BACK, FAR, SIB):
         rows = jnp.where(vis[k] > 0.5, -lt[0:1], LOWEST)
         last = lax.broadcasted_iota(I32, rows.shape, 0) == 7
         meta_out[k] = jnp.where(last, own_loss, rows)
@@ -225,10 +225,10 @@
         )
         cp.start()
         metas[seen_as] = cp
-    qa += [send_q(q_hbm, Y1, Y3, qe, qe, 1), send_q(q_hbm, Y1, Y3, hq, hq, 2)]
-    qb += [send_q(q_hbm, Y3, Y1, hq, qe, 1), send_q(q_hbm, Y3, Y1, 0, hq, 2)]
-    q_back[0].wait_recv()
-    q_far = [send_q(qr.at[FRONT - 1], FAR, SIB, 0, qz, 0)]
+    q_front.append(send_q(q_hbm, BACK, FRONT, qz, nq - qz, 1))
+    q_back.append(send_q(q_hbm, FRONT, BACK, qz, nq - qz, 1))
+    qa.append(send_q(q_hbm, Y1, Y3, hq, hq, 2))
+    qb.append(send_q(q_hbm, Y3, Y1, 0, hq, 2))
 
     for k in range(8):
         @pl.loop(0, 2)
@@ -243,13 +243,14 @@
 
     gp_ref[...] = jnp.dot(wbuf[0:np_, :], q[...], preferred_element_type=F32) * scale
 
-    @pl.loop(0, 2)
-    def _(h):
-        cols = pl.ds(pl.multiple_of(h * hq, hq), hq)
+    def own_gradient(first):
+        cols = pl.ds(first, hq)
         total = tn(wbuf[0:np_, cols], pall[0])
         for k in range(1, 8):
             total = total + tn(wbuf[k * np_ : (k + 1) * np_, cols], pall[k])
         gq_ref[cols, :] = total * scale
+
+    own_gradient(0)
 
     def backward(k, first, rows):
         span = pl.ds(first, rows)
@@ -279,23 +280,24 @@
         return copies
 
     loss_z = spread(zin, z_ss, z_rs, along_z)
-    q_front.append(send_q(q_hbm, BACK, FRONT, qz, nq - qz, 1))
-    q_back.append(send_q(q_hbm, FRONT, BACK, qz, nq - qz, 1))
 
     qa[0].wait_recv()
     ra2 = [send_q(qr.at[Y1 - 1], Y2, Y3, 0, qe, 0)]
     qb[0].wait_recv()
     rb2 = [send_q(qr.at[Y3 - 1], Y2, Y1, nq - qe, qe, 3)]
+    own_gradient(hq)
+    qa[1].wait_recv()
+    ra2 += [send_q(qr.at[Y1 - 1], Y2, Y3, qe + i * qs, qs, 1 + i) for i in range(2)]
+    qb[1].wait_recv()
+    rb2 += [send_q(qr.at[Y3 - 1], Y2, Y1, nq - qe - (i + 1) * qs, qs, 4 + i) for i in range(2)]
     metas[SIB].wait_recv()
     q_sib.wait_recv()
     backward(SIB, 0, hq)
     backward(SIB, hq, hq)
-    qa[1].wait_recv()
-    ra2 += [send_q(qr.at[Y1 - 1], Y2, Y3, qe + i * qs, qs, 1 + i) for i in range(2)]
-    qb[1].wait_recv()
-    rb2 += [send_q(qr.at[Y3 - 1], Y2, Y1, nq - qe - (i + 1) * qs, qs, 4 + i) for i in range(2)]
     backward(Y1, 0, hq)
     backward(Y3, hq, hq)
+    q_back[0].wait_recv()
+    q_far = [send_q(qr.at[FRONT - 1], FAR, SIB, 0, qz, 0)]
     metas[FRONT].wait_recv()
     backward(FRONT, 0, hq)
     metas[BACK].wait_recv()
@@ -345,7 +347,7 @@
     copies = [pltpu.make_async_copy(gq, gq_out, sems.at[0]), pltpu.make_async_copy(gp, gp_out, sems.at[1])]
     for cp in copies:
         cp.start()
-    loss_out[0] = loss[0, 0]
+    loss_out[...] = loss[0, 0:1]
     for cp in copies:
         cp.wait()
 
@@ -414,7 +416,7 @@
             jax.ShapeDtypeStruct((np_, width), F32),
         ),
         in_specs=[inside] * 3,
-        out_specs=(pl.BlockSpec(memory_space=pltpu.SMEM), anywhere, anywhere),
+        out_specs=(inside, anywhere, anywhere),
         scratch_shapes=[dma((2,))],
         compiler_params=pltpu.CompilerParams(vmem_limit_bytes=4 * 2**20),
     )(loss, gq, gp)

time: 60.7 us -> 57.7 us (0.951)
  Pallas kernels: 59.8 us -> 56.8 us
    pallas_call x1, Pallas kernels: 57.8 us -> 54.7 us  [local(): pl.pallas_call(functools.partial(kernel, n_row, n_col, n_z), out_shape=(j...]
where the time goes in v4:
time: 57.7 us; the launch traced here: 57.6 us
  Pallas kernels  56.8 us (98%)
  between operations  0.8 us (1%)
    pallas_call x1, Pallas kernels, local(): pl.pallas_call(functools.partial(kernel, n_row, n_col, n_z), out_shape=(j...  54.7 us
    pallas_call x1, Pallas kernels, local(): pl.pallas_call(finish, out_shape=(jax.ShapeDtypeStruct((1,), F32), jax.Sh...  2.06 us

profile of v4, /device:TPU:1, one launch (start us, length us, event | category | flops | bytes accessed | tf_op | source)
XLA Modules:
  0.0 57.6 jit_solution(9129524511374442974)
XLA Ops:
  0.6 54.7 %shard_map.76 = (f32[8,128]{1,0:T(8,128)S(1)}, f32[512,768]{1,0:T(8,128)S(1)}, f32[384,768]{1,0:T(8,128)S(1)}) custom-call(bf16[512,768]{1,0:T(8,128)(2,1)} %q_hbm.1, bf16[384,768]{1,0:T(8,128)(2,1)} %p_hbm.1, s32[1,512]{1,0:T(1,128)} %bitcast.5, s32[15,512]{1,0:T(8,128)} %bitcast.3, s32[3,512]{1,0:T(4,128)} %bitcast.4), custom_call_target="tpu_custom_call" | custom-call | flops 10000000000 | bytes 10000000 | tf_op jit(solution)/shard_map/pallas_call | solution.py:364
  55.4 2.1 %shard_map.77 = (f32[1]{0:T(128)}, f32[512,768]{1,0:T(8,128)}, f32[384,768]{1,0:T(8,128)}) custom-call(f32[8,128]{1,0:T(8,128)S(1)} %get-tuple-element.6.loss, f32[512,768]{1,0:T(8,128)S(1)} %get-tuple-element.7.gq, f32[384,768]{1,0:T(8,128)S(1)} %get-tuple-element.8.gp), custom_call_target="tpu_custom_call" | custom-call | tf_op jit(solution)/shard_map/pallas_call | solution.py:411

commit v5 on v4

--- a/solution.py
+++ b/solution.py
@@ -68,19 +68,12 @@
     def _():
         pl.semaphore_signal(barrier, inc=1, device_id=even_core, device_id_type=MESH)
 
-    chips = [lax.rem(chip + 2, n_row), lax.rem(chip + n_row - 2, n_row), over_x]
-    chips += [to["row"] - odd for to in along_z.values()]
-    for there in chips:
-        pl.semaphore_signal(barrier, inc=1, device_id={"row": there + 1, "col": c}, device_id_type=MESH)
-
     loads = [
         pltpu.make_async_copy(src, dst, loc_s.at[i])
         for i, (src, dst) in enumerate(
             ((q_hbm, q), (p_hbm, pall.at[OWN]), (bm_hbm, bm), (ro_hbm, ro), (pos_hbm, pos))
         )
     ]
-    for cp in loads:
-        cp.start()
 
     @pl.when(odd == 0)
     def _():
@@ -116,8 +109,15 @@
     pb1 = send_p(p_hbm, Y3, Y1, hp, hp, 1)
     pa1 = send_p(p_hbm, Y1, Y3, hp, hp, 1)
     pb0 = send_p(p_hbm, Y3, Y1, 0, hp, 0)
+    for cp in loads:
+        cp.start()
     p_sib = send_p(p_hbm, SIB, SIB, 0, np_, 0)
     q_sib = send_q(q_hbm, SIB, SIB, 0, nq, 0)
+
+    chips = [lax.rem(chip + 2, n_row), lax.rem(chip + n_row - 2, n_row), over_x]
+    chips += [to["row"] - odd for to in along_z.values()]
+    for there in chips:
+        pl.semaphore_signal(barrier, inc=1, device_id={"row": there + 1, "col": c}, device_id_type=MESH)
 
     @pl.when(odd == 1)
     def _():
@@ -194,7 +194,7 @@
     rb = send_p(pall.at[Y3], Y2, Y1, hp, hp, 1)
     pa1.wait_recv()
     pb0.wait_recv()
-    qe, qs, q0 = nq // 4, nq // 8, nq * 3 // 8
+    q0 = nq * 3 // 8
     qa = [send_q(q_hbm, Y1, Y3, 0, q0, 0), send_q(q_hbm, Y1, Y3, q0, hq - q0, 1)]
     qb = [send_q(q_hbm, Y3, Y1, nq - q0, q0, 0), send_q(q_hbm, Y3, Y1, hq, hq - q0, 1)]
     forward(Y1)
@@ -282,14 +282,14 @@
     loss_z = spread(zin, z_ss, z_rs, along_z)
 
     qa[0].wait_recv()
-    ra2 = [send_q(qr.at[Y1 - 1], Y2, Y3, 0, qe, 0)]
+    ra2 = [send_q(qr.at[Y1 - 1], Y2, Y3, 0, q0, 0)]
     qb[0].wait_recv()
-    rb2 = [send_q(qr.at[Y3 - 1], Y2, Y1, nq - qe, qe, 3)]
+    rb2 = [send_q(qr.at[Y3 - 1], Y2, Y1, nq - q0, q0, 2)]
     own_gradient(hq)
     qa[1].wait_recv()
-    ra2 += [send_q(qr.at[Y1 - 1], Y2, Y3, qe + i * qs, qs, 1 + i) for i in range(2)]
+    ra2.append(send_q(qr.at[Y1 - 1], Y2, Y3, q0, hq - q0, 1))
     qb[1].wait_recv()
-    rb2 += [send_q(qr.at[Y3 - 1], Y2, Y1, nq - qe - (i + 1) * qs, qs, 4 + i) for i in range(2)]
+    rb2.append(send_q(qr.at[Y3 - 1], Y2, Y1, hq, hq - q0, 3))
     metas[SIB].wait_recv()
     q_sib.wait_recv()
     backward(SIB, 0, hq)
@@ -324,30 +324,25 @@
     backward(Y3, 0, hq)
     q_far[1].wait_recv()
     backward(FAR, hq, hq)
-    ra2[0].wait_recv()
-    backward(Y2, 0, qe)
-    rb2[0].wait_recv()
-    backward(Y2, nq - qe, qe)
     for cp in loss_x:
         cp.wait_recv()
     loss_ref[...] = ((xin[0] + xin[1]) + (xin[2] + xin[3])) * (1.0 / (nq * n_row * n_col))
+    ra2[0].wait_recv()
+    backward(Y2, 0, q0)
+    rb2[0].wait_recv()
+    backward(Y2, nq - q0, q0)
     ra2[1].wait_recv()
     rb2[1].wait_recv()
-    backward(Y2, qe, qs)
-    backward(Y2, nq - qe - qs, qs)
-    ra2[2].wait_recv()
-    rb2[2].wait_recv()
-    backward(Y2, hq - qs, 2 * qs)
+    backward(Y2, q0, nq - 2 * q0)
 
     for cp in send_p.sent + send_q.sent + list(metas.values()) + loss_z + loss_x:
         cp.wait_send()
 
 
 def finish(loss, gq, gp, loss_out, gq_out, gp_out, sems):
-    copies = [pltpu.make_async_copy(gq, gq_out, sems.at[0]), pltpu.make_async_copy(gp, gp_out, sems.at[1])]
+    copies = [pltpu.make_async_copy(gq, gq_out, sems.at[0]), pltpu.make_async_copy(gp, gp_out, sems.at[1]), pltpu.make_async_copy(loss.at[pl.ds(0, 1)], loss_out, sems.at[2])]
     for cp in copies:
         cp.start()
-    loss_out[...] = loss[0, 0:1]
     for cp in copies:
         cp.wait()
 
@@ -392,8 +387,8 @@
             dma((5,)),
             dma((10,)),
             dma((8, 2)),
-            dma((19,)),
-            dma((8, 6)),
+            dma((17,)),
+            dma((8, 4)),
             dma((8,)),
             dma((8,)),
             dma((n_z,)),
@@ -408,18 +403,19 @@
         ),
         cost_estimate=pl.CostEstimate(flops=10**10, bytes_accessed=10**7, transcendentals=4 * 10**6),
     )(*(pltpu.with_memory_space_constraint(a, pltpu.HBM) for a in operands))
-    return pl.pallas_call(
+    a, b, d = pl.pallas_call(
         finish,
         out_shape=(
-            jax.ShapeDtypeStruct((1,), F32),
+            jax.ShapeDtypeStruct((1, 128), F32),
             jax.ShapeDtypeStruct((nq, width), F32),
             jax.ShapeDtypeStruct((np_, width), F32),
         ),
         in_specs=[inside] * 3,
-        out_specs=(inside, anywhere, anywhere),
-        scratch_shapes=[dma((2,))],
+        out_specs=(anywhere, anywhere, anywhere),
+        scratch_shapes=[dma((3,))],
         compiler_params=pltpu.CompilerParams(vmem_limit_bytes=4 * 2**20),
     )(loss, gq, gp)
+    return a[0, 0:1], b, d
 
 
 def solution(mesh):

time: 57.7 us -> 57 us (0.988)
  Pallas kernels: 56.8 us -> 56.1 us
where the time goes in v5:
time: 57 us; the launch traced here: 56.9 us
  Pallas kernels  56.1 us (98%)
  between operations  0.8 us (1%)
    pallas_call x1, Pallas kernels, local(): pl.pallas_call(functools.partial(kernel, n_row, n_col, n_z), out_shape=(j...  54.6 us
    pallas_call x1, Pallas kernels, local(): pl.pallas_call(finish, out_shape=(jax.ShapeDtypeStruct((1, 128), F32), ja...  1.56 us

profile of v5, /device:TPU:1, one launch (start us, length us, event | category | flops | bytes accessed | tf_op | source)
XLA Modules:
  0.0 56.9 jit_solution(2474610585410268346)
XLA Ops:
  0.6 54.6 %shard_map.76 = (f32[8,128]{1,0:T(8,128)S(1)}, f32[512,768]{1,0:T(8,128)S(1)}, f32[384,768]{1,0:T(8,128)S(1)}) custom-call(bf16[512,768]{1,0:T(8,128)(2,1)} %q_hbm.1, bf16[384,768]{1,0:T(8,128)(2,1)} %p_hbm.1, s32[1,512]{1,0:T(1,128)} %bitcast.7, s32[15,512]{1,0:T(8,128)} %bitcast.5, s32[3,512]{1,0:T(4,128)} %bitcast.6), custom_call_target="tpu_custom_call" | custom-call | flops 10000000000 | bytes 10000000 | tf_op jit(solution)/shard_map/pallas_call | solution.py:359
  55.2 1.6 %shard_map.77 = (f32[1,128]{1,0:T(1,128)}, f32[512,768]{1,0:T(8,128)}, f32[384,768]{1,0:T(8,128)}) custom-call(f32[8,128]{1,0:T(8,128)S(1)} %get-tuple-element.9.loss, f32[512,768]{1,0:T(8,128)S(1)} %get-tuple-element.10.gq, f32[384,768]{1,0:T(8,128)S(1)} %get-tuple-element.11.gp), custom_call_target="tpu_custom_call" | custom-call | tf_op jit(solution)/shard_map/pallas_call | solution.py:406

commit v6 on v5

--- a/solution.py
+++ b/solution.py
@@ -27,7 +27,7 @@
 def kernel(
     n_row, n_col, n_z,
     q_hbm, p_hbm, pos_hbm, bm_hbm, ro_hbm,
-    loss_ref, gq_ref, gp_ref,
+    loss_ref, gq_ref, gp_ref, p_own, q_tail, m_tail,
     q, pall, qr, pos, bm, ro, vis, ebuf, wbuf, mrow, run_m, run_l, lt, psc, meta_out, meta_in, zin, xin,
     loc_s, p_ss, p_rs, q_ss, q_rs, m_ss, m_rs, z_ss, z_rs, x_ss, x_rs, y_in, z_in,
 ):
@@ -185,6 +185,7 @@
             run_l[0:1, cols] = total
             mrow[k, 0:1, cols] = m_new
 
+    p_own[...] = pall[OWN]
     forward(OWN)
     p_sib.wait_recv()
     forward(SIB)
@@ -327,22 +328,33 @@
     for cp in loss_x:
         cp.wait_recv()
     loss_ref[...] = ((xin[0] + xin[1]) + (xin[2] + xin[3])) * (1.0 / (nq * n_row * n_col))
+    m_tail[...] = meta_in[Y2, :, q0 : nq - q0]
     ra2[0].wait_recv()
     backward(Y2, 0, q0)
     rb2[0].wait_recv()
     backward(Y2, nq - q0, q0)
     ra2[1].wait_recv()
     rb2[1].wait_recv()
-    backward(Y2, q0, nq - 2 * q0)
+    q_tail[...] = qr[Y2 - 1, q0 : nq - q0, :]
 
     for cp in send_p.sent + send_q.sent + list(metas.values()) + loss_z + loss_x:
         cp.wait_send()
 
 
-def finish(loss, gq, gp, loss_out, gq_out, gp_out, sems):
-    copies = [pltpu.make_async_copy(gq, gq_out, sems.at[0]), pltpu.make_async_copy(gp, gp_out, sems.at[1]), pltpu.make_async_copy(loss.at[pl.ds(0, 1)], loss_out, sems.at[2])]
+def finish(loss, gq, gp, p_own, q_tail, m_tail, loss_out, gq_out, gp_out, gp_sum, sems):
+    copies = [
+        pltpu.make_async_copy(gq, gq_out, sems.at[0]),
+        pltpu.make_async_copy(loss.at[pl.ds(0, 1)], loss_out, sems.at[1]),
+    ]
     for cp in copies:
         cp.start()
+    scale = gq.shape[1] ** (-0.5)
+    for b in range(gp.shape[0] // BLK):
+        rows = pl.ds(b * BLK, BLK)
+        w = jnp.exp(nt(p_own[rows, :], q_tail[...]) * scale + m_tail[b : b + 1, :]).astype(BF16)
+        gp_sum[rows, :] = gp[rows, :] + jnp.dot(w, q_tail[...], preferred_element_type=F32) * scale
+        copies.append(pltpu.make_async_copy(gp_sum.at[rows], gp_out.at[rows], sems.at[2 + b]))
+        copies[-1].start()
     for cp in copies:
         cp.wait()
 
@@ -356,15 +368,18 @@
     inside = pl.BlockSpec(memory_space=pltpu.VMEM)
     dma = pltpu.SemaphoreType.DMA
     operands = (queries, passages, positive.reshape(1, nq), block_mask.T, roster.T)
-    loss, gq, gp = pl.pallas_call(
+    loss, gq, *rest = pl.pallas_call(
         functools.partial(kernel, n_row, n_col, n_z),
         out_shape=(
             jax.ShapeDtypeStruct((8, 128), F32),
             jax.ShapeDtypeStruct((nq, width), F32),
             jax.ShapeDtypeStruct((np_, width), F32),
+            jax.ShapeDtypeStruct((np_, width), BF16),
+            jax.ShapeDtypeStruct((nq // 4, width), BF16),
+            jax.ShapeDtypeStruct((8, nq // 4), F32),
         ),
         in_specs=[anywhere] * 5,
-        out_specs=(inside,) * 3,
+        out_specs=(inside,) * 6,
         scratch_shapes=[
             pltpu.VMEM((nq, width), BF16),
             pltpu.VMEM((8, np_, width), BF16),
@@ -410,11 +425,11 @@
             jax.ShapeDtypeStruct((nq, width), F32),
             jax.ShapeDtypeStruct((np_, width), F32),
         ),
-        in_specs=[inside] * 3,
+        in_specs=[inside] * 6,
         out_specs=(anywhere, anywhere, anywhere),
-        scratch_shapes=[dma((3,))],
-        compiler_params=pltpu.CompilerParams(vmem_limit_bytes=4 * 2**20),
-    )(loss, gq, gp)
+        scratch_shapes=[pltpu.VMEM((np_, width), F32), dma((2 + np_ // BLK,))],
+        compiler_params=pltpu.CompilerParams(vmem_limit_bytes=8 * 2**20),
+    )(loss, gq, *rest)
     return a[0, 0:1], b, d
 
 

time: 57 us -> 56.4 us (0.989)
  Pallas kernels: 56.1 us -> 55.5 us
    pallas_call x1, Pallas kernels: 54.6 us -> 53.8 us  [local(): pl.pallas_call(functools.partial(kernel, n_row, n_col, n_z), out_shape=(j...]
where the time goes in v6:
time: 56.4 us; the launch traced here: 56.3 us
  Pallas kernels  55.5 us (98%)
  between operations  0.8 us (1%)
    pallas_call x1, Pallas kernels, local(): pl.pallas_call(functools.partial(kernel, n_row, n_col, n_z), out_shape=(j...  53.8 us
    pallas_call x1, Pallas kernels, local(): pl.pallas_call(finish, out_shape=(jax.ShapeDtypeStruct((1, 128), F32), ja...  1.66 us

profile of v6, /device:TPU:1, one launch (start us, length us, event | category | flops | bytes accessed | tf_op | source)
XLA Modules:
  0.0 56.3 jit_solution(15749844792049657170)
XLA Ops:
  0.6 53.8 %shard_map.76 = (f32[8,128]{1,0:T(8,128)S(1)}, f32[512,768]{1,0:T(8,128)S(1)}, f32[384,768]{1,0:T(8,128)S(1)}, bf16[384,768]{1,0:T(8,128)(2,1)S(1)}, bf16[128,768]{1,0:T(8,128)(2,1)S(1)}, /*index=5*/f32[8,128]{1,0:T(8,128)S(1)}) custom-call(bf16[512,768]{1,0:T(8,128)(2,1)} %q_hbm.1, bf16[384,768]{1,0:T(8,128)(2,1)} %p_hbm.1, s32[1,512]{1,0:T(1,128)} %bitcast.7, ...), custom_call_target="tpu_custom_call" | custom-call | flops 10000000000 | bytes 10000000 | tf_op jit(solution)/shard_map/pallas_call | solution.py:371
  54.4 1.7 %shard_map.77 = (f32[1,128]{1,0:T(1,128)}, f32[512,768]{1,0:T(8,128)}, f32[384,768]{1,0:T(8,128)}) custom-call(f32[8,128]{1,0:T(8,128)S(1)} %get-tuple-element.12.loss, f32[512,768]{1,0:T(8,128)S(1)} %get-tuple-element.13.gq, f32[384,768]{1,0:T(8,128)S(1)} %get-tuple-element.14.gp, bf16[384,768]{1,0:T(8,128)(2,1)S(1)} %get-tuple-element.15.p_own, ...), custom_call_target="tpu_custom_call" | custom-call | tf_op jit(solution)/shard_map/pallas_call | solution.py:421

commit v7 on v6

--- a/solution.py
+++ b/solution.py
@@ -195,7 +195,7 @@
     rb = send_p(pall.at[Y3], Y2, Y1, hp, hp, 1)
     pa1.wait_recv()
     pb0.wait_recv()
-    q0 = nq * 3 // 8
+    q0 = nq * 7 // 16
     qa = [send_q(q_hbm, Y1, Y3, 0, q0, 0), send_q(q_hbm, Y1, Y3, q0, hq - q0, 1)]
     qb = [send_q(q_hbm, Y3, Y1, nq - q0, q0, 0), send_q(q_hbm, Y3, Y1, hq, hq - q0, 1)]
     forward(Y1)
@@ -375,8 +375,8 @@
             jax.ShapeDtypeStruct((nq, width), F32),
             jax.ShapeDtypeStruct((np_, width), F32),
             jax.ShapeDtypeStruct((np_, width), BF16),
-            jax.ShapeDtypeStruct((nq // 4, width), BF16),
-            jax.ShapeDtypeStruct((8, nq // 4), F32),
+            jax.ShapeDtypeStruct((nq // 8, width), BF16),
+            jax.ShapeDtypeStruct((8, nq // 8), F32),
         ),
         in_specs=[anywhere] * 5,
         out_specs=(inside,) * 6,

time: 56.4 us -> 56.9 us (level)
  no operation moved by 1% of the time
where the time goes in v7:
time: 56.9 us; the launch traced here: 56.8 us
  Pallas kernels  56 us (98%)
  between operations  0.8 us (1%)
    pallas_call x1, Pallas kernels, local(): pl.pallas_call(functools.partial(kernel, n_row, n_col, n_z), out_shape=(j...  54.4 us
    pallas_call x1, Pallas kernels, local(): pl.pallas_call(finish, out_shape=(jax.ShapeDtypeStruct((1, 128), F32), ja...  1.65 us

profile of v7, /device:TPU:1, one launch (start us, length us, event | category | flops | bytes accessed | tf_op | source)
XLA Modules:
  0.0 56.8 jit_solution(8053848888113719708)
XLA Ops:
  0.6 54.4 %shard_map.76 = (f32[8,128]{1,0:T(8,128)S(1)}, f32[512,768]{1,0:T(8,128)S(1)}, f32[384,768]{1,0:T(8,128)S(1)}, bf16[384,768]{1,0:T(8,128)(2,1)S(1)}, bf16[64,768]{1,0:T(8,128)(2,1)S(1)}, /*index=5*/f32[8,64]{1,0:T(8,128)S(1)}) custom-call(bf16[512,768]{1,0:T(8,128)(2,1)} %q_hbm.1, bf16[384,768]{1,0:T(8,128)(2,1)} %p_hbm.1, s32[1,512]{1,0:T(1,128)} %bitcast.7, ...), custom_call_target="tpu_custom_call" | custom-call | flops 10000000000 | bytes 10000000 | tf_op jit(solution)/shard_map/pallas_call | solution.py:371
  55.0 1.6 %shard_map.77 = (f32[1,128]{1,0:T(1,128)}, f32[512,768]{1,0:T(8,128)}, f32[384,768]{1,0:T(8,128)}) custom-call(f32[8,128]{1,0:T(8,128)S(1)} %get-tuple-element.12.loss, f32[512,768]{1,0:T(8,128)S(1)} %get-tuple-element.13.gq, f32[384,768]{1,0:T(8,128)S(1)} %get-tuple-element.14.gp, bf16[384,768]{1,0:T(8,128)(2,1)S(1)} %get-tuple-element.15.p_own, ...), custom_call_target="tpu_custom_call" | custom-call | tf_op jit(solution)/shard_map/pallas_call | solution.py:421
